TPU v7x, 32 devices: a whole 2x2x4 slice. The times are simulated.
32 devices in a mesh: group: 4 (over y, x), shard: 8 (over z, core).
Axes of the slice: x: 2, y: 2, z: 4, core: 2. Of those that a mesh axis runs over, the one named last changes fastest.
Arguments:
- features: bfloat16 [131072, 100], P(('group', 'shard')), may hold values from -6 to 6
- node_counts: int32 [32], P(('group', 'shard')), may hold values from 2048 to 4096, as said below
- degrees: int32 [131072], P(('group', 'shard')), may hold values from 1 to 16, as said below
- neighbours: int32 [131072, 16], P(('group', 'shard')), may hold values from 0 to 4479, as said below
- send_rows: int32 [1024, 12], P(('group', 'shard')), may hold values from 0 to 4095, as said below
- labels: int32 [131072], P(('group', 'shard')), may hold values from 0 to 46
- train_mask: int32 [131072], P(('group', 'shard')), may hold values from 0 to 1
- weight_first: float32 [200, 256], P(None, 'shard'), may hold values from -0.4375 to 0.4375
- weight_rest: float32 [2, 512, 256], P(None, None, 'shard'), may hold values from -0.25 to 0.25
- weight_head: float32 [256, 47], P('shard'), may hold values from -0.375 to 0.375
- biases: float32 [3, 256], P(None, 'shard'), may hold values from -4 to 4
- gains: float32 [3, 256], P(None, 'shard')
- moment_first: float32 [200, 256], P(None, 'shard'), may hold values from -1.9073486e-05 to 1.9073486e-05
- square_first: float32 [200, 256], P(None, 'shard'), may hold values from 1.2235708e-12 to 4.8942833e-12
- moment_rest: float32 [2, 512, 256], P(None, None, 'shard'), may hold values from -5.340576e-05 to 5.340576e-05
- square_rest: float32 [2, 512, 256], P(None, None, 'shard'), may hold values from 1.2235709e-11 to 4.8942836e-11
- moment_head: float32 [256, 47], P('shard'), may hold values from -5.340576e-05 to 5.340576e-05
- square_head: float32 [256, 47], P('shard'), may hold values from 1.2235709e-11 to 4.8942836e-11
- moment_bias: float32 [3, 256], P(None, 'shard'), may hold values from -0.00015258789 to 0.00015258789
- square_bias: float32 [3, 256], P(None, 'shard'), may hold values from 1.1012138e-10 to 4.404855e-10
- moment_gain: float32 [3, 256], P(None, 'shard'), may hold values from -0.00015258789 to 0.00015258789
- square_gain: float32 [3, 256], P(None, 'shard'), may hold values from 1.1012138e-10 to 4.404855e-10
Outputs:
- loss_sum: float32 [], replicated
- label_count: float32 [], replicated
- grad_norm: float32 [], replicated
- new_first: float32 [200, 256], P(None, 'shard')
- new_moment_first: float32 [200, 256], P(None, 'shard')
- new_square_first: float32 [200, 256], P(None, 'shard')
- new_rest: float32 [2, 512, 256], P(None, None, 'shard')
- new_moment_rest: float32 [2, 512, 256], P(None, None, 'shard')
- new_square_rest: float32 [2, 512, 256], P(None, None, 'shard')
- new_head: float32 [256, 47], P('shard')
- new_moment_head: float32 [256, 47], P('shard')
- new_square_head: float32 [256, 47], P('shard')
- new_biases: float32 [3, 256], P(None, 'shard')
- new_moment_bias: float32 [3, 256], P(None, 'shard')
- new_square_bias: float32 [3, 256], P(None, 'shard')
- new_gains: float32 [3, 256], P(None, 'shard')
- new_moment_gain: float32 [3, 256], P(None, 'shard')
- new_square_gain: float32 [3, 256], P(None, 'shard')
- copy_first: bfloat16 [200, 256], P(None, 'shard')
- copy_rest: bfloat16 [2, 512, 256], P(None, None, 'shard')
- copy_head: bfloat16 [256, 47], P('shard')
Inputs may be any that keep to these rules, and one draw needn't show every extreme that they name: `node_counts`: between half of 4096 and 4096; some device holds exactly 4096 nodes. `degrees`: some node uses all 16 slots. `neighbours`: for a counted slot's device d, each used neighbour column is either an own row below node_counts[d] or a received row at 4096 or above; unused slots hold any column. `send_rows`: each entry is below node_counts of the sending device; the largest value is reached.
All inputs are finite; a program needn't handle non-finite values.
Results may differ from a plain program's by a relative error of at most 0.0083.
Values may be sent and summed in bfloat16 or wider, within the bound.
A program may use at most 320 MiB of HBM per device.

v0:
```python
import jax
import jax.numpy as jnp
from jax import lax
from jax.sharding import PartitionSpec as P

STEP = 10


norm_epsilon = 1e-05
threshold = 0.002
beta_one = 0.5
beta_two = 0.5
adam_epsilon = 1e-08


def neighbour_table(neigh_block, degree_block, columns):
    positions = lax.broadcasted_iota(jnp.int32, (neigh_block.shape[0], columns), 1)
    counts = jnp.zeros((neigh_block.shape[0], columns), jnp.bfloat16)
    for neighbour_slot in range(neigh_block.shape[1]):
        matched = (neigh_block[:, neighbour_slot : neighbour_slot + 1] == positions) & (
            degree_block[:, None] > neighbour_slot
        )
        counts = counts + matched.astype(jnp.bfloat16)
    return counts


def build_tables(neigh_blocks, degree_blocks, columns):

    def build_one_block(operands):
        neigh_block, degree_block = operands
        return neighbour_table(neigh_block, degree_block, columns)

    return lax.map(build_one_block, (neigh_blocks, degree_blocks))


def aggregate_forward(table_low, count_blocks):

    def aggregate_one_block(ones_table):
        return jnp.dot(ones_table, table_low, preferred_element_type=jnp.float32)

    summed_rows = lax.map(aggregate_one_block, count_blocks)
    return summed_rows.reshape(-1, table_low.shape[1])


def aggregate_backward(grad_low, count_blocks):
    grad_blocks = grad_low.reshape(count_blocks.shape[0], count_blocks.shape[1], grad_low.shape[1])

    def add_block(carried, operands):
        ones_table, grad_block = operands
        added = lax.dot_general(
            ones_table, grad_block, (((0,), (0,)), ((), ())), preferred_element_type=jnp.float32
        )
        return (carried + added, None)

    start = jnp.zeros((count_blocks.shape[2], grad_low.shape[1]), jnp.float32)
    result, unused = lax.scan(add_block, start, (count_blocks, grad_blocks))
    return result


def move_rows(outgoing, per_peer, forward):
    devices = outgoing.shape[0] // per_peer
    feature = outgoing.shape[1]
    if forward:
        arrived = lax.all_to_all(
            outgoing.reshape(devices, per_peer, feature),
            ("group", "shard"),
            split_axis=0,
            concat_axis=0,
            tiled=True,
        )
    else:
        arrived = lax.all_to_all(
            outgoing.reshape(devices, per_peer, feature),
            ("group", "shard"),
            split_axis=0,
            concat_axis=0,
            tiled=True,
        )
    return arrived.reshape(devices * per_peer, feature)


def layer_forward(inputs_low, weight_low, bias_low, gain_low, graph):
    count_blocks, degree_column, send_rows = graph
    outgoing = jnp.take(inputs_low, send_rows.reshape(-1), axis=0)
    received = move_rows(outgoing, send_rows.shape[1], True)
    table_low = jnp.concatenate([inputs_low, received], axis=0)
    summed_rows = aggregate_forward(table_low, count_blocks)
    mean_low = (summed_rows / degree_column).astype(jnp.bfloat16)
    joined = jnp.concatenate([inputs_low, mean_low], axis=1)
    before = jnp.dot(joined, weight_low, preferred_element_type=jnp.float32) + bias_low.astype(
        jnp.float32
    )
    activity = jax.nn.silu(before)
    inverse_rms = lax.rsqrt(jnp.mean(activity * activity, axis=1, keepdims=True) + norm_epsilon)
    hidden = gain_low.astype(jnp.float32) * (activity * inverse_rms)
    return (hidden, (joined, before))


def layer_backward(grad_hidden, kept, weight_low, gain_low, graph, need_input):
    joined, before = kept
    count_blocks, degree_column, send_rows = graph
    sigmoid_value = jax.nn.sigmoid(before)
    activity = before * sigmoid_value
    inverse_rms = lax.rsqrt(jnp.mean(activity * activity, axis=1, keepdims=True) + norm_epsilon)
    normalized = activity * inverse_rms
    grad_gain = jnp.sum(grad_hidden * normalized, axis=0)
    upstream = grad_hidden * gain_low.astype(jnp.float32)
    grad_activity = inverse_rms * (
        upstream - normalized * jnp.mean(upstream * normalized, axis=1, keepdims=True)
    )
    grad_before = (grad_activity * sigmoid_value * (1.0 + before * (1.0 - sigmoid_value))).astype(
        jnp.bfloat16
    )
    grad_bias = jnp.sum(grad_before.astype(jnp.float32), axis=0)
    grad_weight = lax.dot_general(
        joined, grad_before, (((0,), (0,)), ((), ())), preferred_element_type=jnp.float32
    )
    if not need_input:
        return (None, grad_weight, grad_bias, grad_gain)
    grad_joined = lax.dot_general(
        grad_before, weight_low, (((1,), (1,)), ((), ())), preferred_element_type=jnp.float32
    )
    width = joined.shape[1] // 2
    owned_nodes = joined.shape[0]
    grad_mean_low = (grad_joined[:, width:] / degree_column).astype(jnp.bfloat16)
    grad_table = aggregate_backward(grad_mean_low, count_blocks)
    grad_remote = grad_table[owned_nodes:].astype(jnp.bfloat16)
    arrived = move_rows(grad_remote, send_rows.shape[1], False)
    returned = jax.ops.segment_sum(
        arrived.astype(jnp.float32), send_rows.reshape(-1), num_segments=owned_nodes
    )
    grad_input = grad_joined[:, :width] + grad_table[:owned_nodes] + returned
    return (grad_input, grad_weight, grad_bias, grad_gain)


def adamw(weight, grad, moment, square, rate, decay):
    moment_new = beta_one * moment + (1.0 - beta_one) * grad
    square_new = beta_two * square + (1.0 - beta_two) * grad * grad
    moment_hat = moment_new / (1.0 - beta_one**STEP)
    square_hat = square_new / (1.0 - beta_two**STEP)
    weight_new = weight - rate * (
        moment_hat / (jnp.sqrt(square_hat) + adam_epsilon) + decay * weight
    )
    return (weight_new, moment_new, square_new)


def per_device(
    features,
    node_counts,
    degrees,
    neighbours,
    send_rows,
    labels,
    train_mask,
    weight_first,
    weight_rest,
    weight_head,
    biases,
    gains,
    moment_first,
    square_first,
    moment_rest,
    square_rest,
    moment_head,
    square_head,
    moment_bias,
    square_bias,
    moment_gain,
    square_gain,
):
    gathered = (
        lax.all_gather(weight_first.astype(jnp.bfloat16), "shard", axis=1, tiled=True),
        lax.all_gather(weight_rest.astype(jnp.bfloat16), "shard", axis=2, tiled=True),
        lax.all_gather(weight_head.astype(jnp.bfloat16), "shard", axis=0, tiled=True),
        lax.all_gather(biases.astype(jnp.bfloat16), "shard", axis=1, tiled=True),
        lax.all_gather(gains.astype(jnp.bfloat16), "shard", axis=1, tiled=True),
    )
    first_low, rest_low, head_low, bias_low, gain_low = gathered
    owned_nodes = features.shape[0]
    block = min(512, owned_nodes)
    neigh_blocks = neighbours.reshape(owned_nodes // block, block, neighbours.shape[1])
    degree_blocks = degrees.reshape(owned_nodes // block, block)
    degree_column = degrees.astype(jnp.float32)[:, None]
    count_blocks = build_tables(neigh_blocks, degree_blocks, owned_nodes + send_rows.size)
    graph = (count_blocks, degree_column, send_rows)
    layer_weights = [first_low] + [rest_low[level] for level in range(rest_low.shape[0])]
    hidden_low = features
    kept_layers = []
    for level in range(len(layer_weights)):
        hidden, kept = layer_forward(
            hidden_low, layer_weights[level], bias_low[level], gain_low[level], graph
        )
        kept_layers.append(kept)
        hidden_low = hidden.astype(jnp.bfloat16)
    logits = jnp.dot(hidden_low, head_low, preferred_element_type=jnp.float32)
    logp = jax.nn.log_softmax(logits, axis=1)
    classes = lax.broadcasted_iota(jnp.int32, logits.shape, 1)
    labels_hot = (labels[:, None] == classes).astype(jnp.float32)
    rows_index = lax.broadcasted_iota(jnp.int32, (owned_nodes,), 0)
    counted = ((rows_index < node_counts[0]) & (train_mask > 0)).astype(jnp.float32)
    local_loss = -jnp.sum(jnp.sum(logp * labels_hot, axis=1) * counted)
    loss_sum, label_count = lax.psum((local_loss, jnp.sum(counted)), ("group", "shard"))
    grad_logits = ((jnp.exp(logp) - labels_hot) * (counted / label_count)[:, None]).astype(
        jnp.bfloat16
    )
    grad_head = lax.dot_general(
        hidden_low, grad_logits, (((0,), (0,)), ((), ())), preferred_element_type=jnp.float32
    )
    grad_hidden = lax.dot_general(
        grad_logits, head_low, (((1,), (1,)), ((), ())), preferred_element_type=jnp.float32
    )
    weight_grads = [None] * len(layer_weights)
    bias_grads = [None] * len(layer_weights)
    gain_grads = [None] * len(layer_weights)
    for level in reversed(range(len(layer_weights))):
        grad_hidden, weight_grads[level], bias_grads[level], gain_grads[level] = layer_backward(
            grad_hidden, kept_layers[level], layer_weights[level], gain_low[level], graph, level > 0
        )
    local_grads = (
        weight_grads[0],
        jnp.stack(weight_grads[1:]),
        grad_head,
        jnp.stack(bias_grads),
        jnp.stack(gain_grads),
    )
    split = (
        lax.psum_scatter(local_grads[0], "shard", scatter_dimension=1, tiled=True),
        lax.psum_scatter(local_grads[1], "shard", scatter_dimension=2, tiled=True),
        lax.psum_scatter(local_grads[2], "shard", scatter_dimension=0, tiled=True),
        lax.psum_scatter(local_grads[3], "shard", scatter_dimension=1, tiled=True),
        lax.psum_scatter(local_grads[4], "shard", scatter_dimension=1, tiled=True),
    )
    summed_rows = lax.psum((split[0], split[1], split[2], split[3], split[4]), "group")
    squares = sum((jnp.sum(member * member) for member in summed_rows))
    total_square = lax.psum(squares, "shard")
    grad_norm = jnp.sqrt(total_square)
    factor = jnp.minimum(1.0, threshold / grad_norm)
    clipped = [member * factor for member in summed_rows]
    first_out = adamw(weight_first, clipped[0], moment_first, square_first, 0.05, 0.01)
    rest_out = adamw(weight_rest, clipped[1], moment_rest, square_rest, 0.05, 0.01)
    head_out = adamw(weight_head, clipped[2], moment_head, square_head, 0.05, 0.01)
    bias_out = adamw(biases, clipped[3], moment_bias, square_bias, 0.3, 0.0)
    gain_out = adamw(gains, clipped[4], moment_gain, square_gain, 0.3, 0.0)
    return (
        loss_sum,
        label_count,
        grad_norm,
        first_out[0],
        first_out[1],
        first_out[2],
        rest_out[0],
        rest_out[1],
        rest_out[2],
        head_out[0],
        head_out[1],
        head_out[2],
        bias_out[0],
        bias_out[1],
        bias_out[2],
        gain_out[0],
        gain_out[1],
        gain_out[2],
        first_out[0].astype(jnp.bfloat16),
        rest_out[0].astype(jnp.bfloat16),
        head_out[0].astype(jnp.bfloat16),
    )


def solution(mesh):
    return jax.shard_map(
        per_device,
        mesh=mesh,
        in_specs=(
            P(("group", "shard"), None),
            P(("group", "shard")),
            P(("group", "shard")),
            P(("group", "shard"), None),
            P(("group", "shard"), None),
            P(("group", "shard")),
            P(("group", "shard")),
            P(None, "shard"),
            P(None, None, "shard"),
            P("shard", None),
            P(None, "shard"),
            P(None, "shard"),
            P(None, "shard"),
            P(None, "shard"),
            P(None, None, "shard"),
            P(None, None, "shard"),
            P("shard", None),
            P("shard", None),
            P(None, "shard"),
            P(None, "shard"),
            P(None, "shard"),
            P(None, "shard"),
        ),
        out_specs=(
            P(),
            P(),
            P(),
            P(None, "shard"),
            P(None, "shard"),
            P(None, "shard"),
            P(None, None, "shard"),
            P(None, None, "shard"),
            P(None, None, "shard"),
            P("shard", None),
            P("shard", None),
            P("shard", None),
            P(None, "shard"),
            P(None, "shard"),
            P(None, "shard"),
            P(None, "shard"),
            P(None, "shard"),
            P(None, "shard"),
            P(None, "shard"),
            P(None, None, "shard"),
            P("shard", None),
        ),
        check_vma=False,
    )
```

profile of v0, /device:TPU:0, one launch (start us, length us, event | category | flops | bytes accessed | tf_op | source)
XLA Modules:
  0.0 1103.8 jit_solution(114506167951374928)
XLA Ops:
  12.8 7.3 all-to-all-start
  22.4 12.0 %all-gather.1 = bf16[8,32,3]{1,2,0:T(4,128)(2,1)S(1)} all-gather(bf16[1,32,3]{1,2,0:T(4,128)(2,1)S(1)} %convert_bitcast_fusion), channel_id=1, replica_groups=mesh['group'=4,'shard'=8] {'shard'}, dimensions={0}, use_global_device_ids=true | all-gather | bytes 1728 | tf_op jit(solution)/shard_map/all_gather | solution.py:175
  35.6 308.0 %while.62 = (s32[]{:T(128)}, bf16[8,512,4480]{2,1,0:T(8,128)(2,1)}, s32[8,512,16]{1,0,2:T(8,128)S(1)}, s32[8,512]{1,0:T(8,128)S(1)}, s32[]{:T(128)}) while((s32[]{:T(128)}, bf16[8,512,4480]{2,1,0:T(8,128)(2,1)}, s32[8,512,16]{1,0,2:T(8,128)S(1)}, s32[8,512]{1,0:T(8,128)S(1)}, s32[]{:T(128)}) %tuple.205), condition=%wide.region_1.2_spmd, body=%wide.region_0.1_spmd.sunk | while | flops 183508992 | bytes 4835409 | solution.py:33
  35.9 38.3 %fusion.154 = bf16[8,512,4480]{2,1,0:T(8,128)(2,1)} fusion(bf16[8,512,4480]{2,1,0:T(8,128)(2,1)} %get-tuple-element.622, s32[]{:T(128)S(6)} %copy.142, s32[512]{0:T(512)S(1)} %bitcast.212, s32[512]{0:T(512)S(1)} %bitcast.213, s32[512]{0:T(512)S(1)} %bitcast.214, s32[512]{0:T(512)S(1)} %bitcast.215, s32[512]{0:T(512)S(1)} %bitcast.216, ...), kind=kLoop, calls=%fused_computation.83.clone.1 | loop fusion | flops 183500800 | bytes 4628484 | tf_op jit(solution)/shard_map/while/body/jit(dynamic_update_index_in_dim)/dynamic_update_slice | solution.py:33
  74.3 38.3 %fusion.154 = bf16[8,512,4480]{2,1,0:T(8,128)(2,1)} fusion(bf16[8,512,4480]{2,1,0:T(8,128)(2,1)} %get-tuple-element.622, s32[]{:T(128)S(6)} %copy.142, s32[512]{0:T(512)S(1)} %bitcast.212, s32[512]{0:T(512)S(1)} %bitcast.213, s32[512]{0:T(512)S(1)} %bitcast.214, s32[512]{0:T(512)S(1)} %bitcast.215, s32[512]{0:T(512)S(1)} %bitcast.216, ...), kind=kLoop, calls=%fused_computation.83.clone.1 | loop fusion | flops 183500800 | bytes 4628484 | tf_op jit(solution)/shard_map/while/body/jit(dynamic_update_index_in_dim)/dynamic_update_slice | solution.py:33
  112.8 38.3 %fusion.154 = bf16[8,512,4480]{2,1,0:T(8,128)(2,1)} fusion(bf16[8,512,4480]{2,1,0:T(8,128)(2,1)} %get-tuple-element.622, s32[]{:T(128)S(6)} %copy.142, s32[512]{0:T(512)S(1)} %bitcast.212, s32[512]{0:T(512)S(1)} %bitcast.213, s32[512]{0:T(512)S(1)} %bitcast.214, s32[512]{0:T(512)S(1)} %bitcast.215, s32[512]{0:T(512)S(1)} %bitcast.216, ...), kind=kLoop, calls=%fused_computation.83.clone.1 | loop fusion | flops 183500800 | bytes 4628484 | tf_op jit(solution)/shard_map/while/body/jit(dynamic_update_index_in_dim)/dynamic_update_slice | solution.py:33
  151.4 38.3 %fusion.154 = bf16[8,512,4480]{2,1,0:T(8,128)(2,1)} fusion(bf16[8,512,4480]{2,1,0:T(8,128)(2,1)} %get-tuple-element.622, s32[]{:T(128)S(6)} %copy.142, s32[512]{0:T(512)S(1)} %bitcast.212, s32[512]{0:T(512)S(1)} %bitcast.213, s32[512]{0:T(512)S(1)} %bitcast.214, s32[512]{0:T(512)S(1)} %bitcast.215, s32[512]{0:T(512)S(1)} %bitcast.216, ...), kind=kLoop, calls=%fused_computation.83.clone.1 | loop fusion | flops 183500800 | bytes 4628484 | tf_op jit(solution)/shard_map/while/body/jit(dynamic_update_index_in_dim)/dynamic_update_slice | solution.py:33
  189.9 38.3 %fusion.154 = bf16[8,512,4480]{2,1,0:T(8,128)(2,1)} fusion(bf16[8,512,4480]{2,1,0:T(8,128)(2,1)} %get-tuple-element.622, s32[]{:T(128)S(6)} %copy.142, s32[512]{0:T(512)S(1)} %bitcast.212, s32[512]{0:T(512)S(1)} %bitcast.213, s32[512]{0:T(512)S(1)} %bitcast.214, s32[512]{0:T(512)S(1)} %bitcast.215, s32[512]{0:T(512)S(1)} %bitcast.216, ...), kind=kLoop, calls=%fused_computation.83.clone.1 | loop fusion | flops 183500800 | bytes 4628484 | tf_op jit(solution)/shard_map/while/body/jit(dynamic_update_index_in_dim)/dynamic_update_slice | solution.py:33
  228.3 38.3 %fusion.154 = bf16[8,512,4480]{2,1,0:T(8,128)(2,1)} fusion(bf16[8,512,4480]{2,1,0:T(8,128)(2,1)} %get-tuple-element.622, s32[]{:T(128)S(6)} %copy.142, s32[512]{0:T(512)S(1)} %bitcast.212, s32[512]{0:T(512)S(1)} %bitcast.213, s32[512]{0:T(512)S(1)} %bitcast.214, s32[512]{0:T(512)S(1)} %bitcast.215, s32[512]{0:T(512)S(1)} %bitcast.216, ...), kind=kLoop, calls=%fused_computation.83.clone.1 | loop fusion | flops 183500800 | bytes 4628484 | tf_op jit(solution)/shard_map/while/body/jit(dynamic_update_index_in_dim)/dynamic_update_slice | solution.py:33
  266.8 38.3 %fusion.154 = bf16[8,512,4480]{2,1,0:T(8,128)(2,1)} fusion(bf16[8,512,4480]{2,1,0:T(8,128)(2,1)} %get-tuple-element.622, s32[]{:T(128)S(6)} %copy.142, s32[512]{0:T(512)S(1)} %bitcast.212, s32[512]{0:T(512)S(1)} %bitcast.213, s32[512]{0:T(512)S(1)} %bitcast.214, s32[512]{0:T(512)S(1)} %bitcast.215, s32[512]{0:T(512)S(1)} %bitcast.216, ...), kind=kLoop, calls=%fused_computation.83.clone.1 | loop fusion | flops 183500800 | bytes 4628484 | tf_op jit(solution)/shard_map/while/body/jit(dynamic_update_index_in_dim)/dynamic_update_slice | solution.py:33
  305.3 38.3 %fusion.154 = bf16[8,512,4480]{2,1,0:T(8,128)(2,1)} fusion(bf16[8,512,4480]{2,1,0:T(8,128)(2,1)} %get-tuple-element.622, s32[]{:T(128)S(6)} %copy.142, s32[512]{0:T(512)S(1)} %bitcast.212, s32[512]{0:T(512)S(1)} %bitcast.213, s32[512]{0:T(512)S(1)} %bitcast.214, s32[512]{0:T(512)S(1)} %bitcast.215, s32[512]{0:T(512)S(1)} %bitcast.216, ...), kind=kLoop, calls=%fused_computation.83.clone.1 | loop fusion | flops 183500800 | bytes 4628484 | tf_op jit(solution)/shard_map/while/body/jit(dynamic_update_index_in_dim)/dynamic_update_slice | solution.py:33
  343.7 8.7 all-gather
  353.1 14.0 %all_gather.16 = bf16[200,256]{0,1:T(8,128)(2,1)S(1)} all-gather(bf16[200,32]{0,1:T(8,128)(2,1)S(1)} %convert_element_type.270), channel_id=1, replica_groups=mesh['group'=4,'shard'=8] {'shard'}, dimensions={1}, use_global_device_ids=true | all-gather | bytes 115200 | tf_op jit(solution)/shard_map/all_gather | solution.py:172
  368.3 52.8 %while.63 = (s32[]{:T(128)}, f32[8,512,100]{1,0,2:T(8,128)S(1)}, bf16[8,512,4480]{2,1,0:T(8,128)(2,1)}, bf16[4480,100]{1,0:T(8,128)(2,1)}, s32[]{:T(128)}, /*index=5*/s32[]{:T(128)}) while((s32[]{:T(128)}, f32[8,512,100]{1,0,2:T(8,128)S(1)}, bf16[8,512,4480]{2,1,0:T(8,128)(2,1)}, bf16[4480,100]{1,0:T(8,128)(2,1)}, s32[]{:T(128)}, ...), condition=%wide.region_3.4_spmd, body=%wide.region_2.3_spmd.sunk | while | flops 458752000 | bytes 6758485 | solution.py:41
  434.8 18.4 %all_gather.18 = bf16[2,512,256]{1,2,0:T(8,128)(2,1)S(1)} all-gather(bf16[2,512,32]{1,2,0:T(8,128)(2,1)S(1)} %convert_element_type.274), channel_id=1, replica_groups=mesh['group'=4,'shard'=8] {'shard'}, dimensions={2}, use_global_device_ids=true | all-gather | bytes 589824 | tf_op jit(solution)/shard_map/all_gather | solution.py:173
  457.1 41.9 %while.64 = (s32[]{:T(128)}, f32[8,512,256]{2,1,0:T(8,128)}, bf16[8,512,4480]{2,1,0:T(8,128)(2,1)}, bf16[4480,256]{1,0:T(8,128)(2,1)}, s32[]{:T(128)}) while((s32[]{:T(128)}, f32[8,512,256]{2,1,0:T(8,128)}, bf16[8,512,4480]{2,1,0:T(8,128)(2,1)}, bf16[4480,256]{1,0:T(8,128)(2,1)}, s32[]{:T(128)}) %tuple.199), condition=%wide.region_6.8_spmd, body=%wide.region_5.7_spmd.sunk | while | flops 1174405120 | bytes 7406661 | solution.py:41
  457.1 5.2 fusion.160
  467.6 5.2 fusion.160
  472.8 5.2 fusion.160
  478.1 5.2 fusion.160
  483.3 5.2 fusion.160
  493.7 5.2 fusion.160
  517.2 15.0 %all_gather.19 = bf16[256,47]{1,0:T(8,128)(2,1)S(1)} all-gather(bf16[32,47]{1,0:T(8,128)(2,1)S(1)} %convert_element_type.278), channel_id=1, replica_groups=mesh['group'=4,'shard'=8] {'shard'}, dimensions={0}, use_global_device_ids=true | all-gather | bytes 27072 | tf_op jit(solution)/shard_map/all_gather | solution.py:174
  537.8 41.8 %while.65 = (s32[]{:T(128)}, f32[8,512,256]{2,1,0:T(8,128)}, bf16[8,512,4480]{2,1,0:T(8,128)(2,1)}, bf16[4480,256]{1,0:T(8,128)(2,1)}, s32[]{:T(128)}) while((s32[]{:T(128)}, f32[8,512,256]{2,1,0:T(8,128)}, bf16[8,512,4480]{2,1,0:T(8,128)(2,1)}, bf16[4480,256]{1,0:T(8,128)(2,1)}, s32[]{:T(128)}) %tuple.200), condition=%wide.region_9.11_spmd, body=%wide.region_8.10_spmd.sunk | while | flops 1174405120 | bytes 7406661 | solution.py:41
  537.9 5.2 fusion.163
  553.5 5.2 fusion.163
  563.9 5.2 fusion.163
  574.4 5.2 fusion.163
  588.9 40.2 %all-reduce.1 = (f32[]{:T(128)}, f32[]{:T(128)}) all-reduce(f32[]{:T(128)} %get-tuple-element.287, f32[]{:T(128)S(6)} %neg.19), channel_id=1, replica_groups=mesh['group'=4,'shard'=8] {'group','shard'}, use_global_device_ids=true, to_apply=%region_17.19 | all-reduce | flops 2 | bytes 16 | tf_op jit(solution)/shard_map/psum | solution.py:202
  630.5 5.7 multiply_reduce_fusion
  646.2 56.8 %while.66 = (s32[]{:T(128)}, f32[4480,256]{1,0:T(8,128)}, bf16[8,512,4480]{2,1,0:T(8,128)(2,1)}, bf16[8,512,256]{2,1,0:T(8,128)(2,1)}, s32[]{:T(128)}, /*index=5*/s32[]{:T(128)}) while((s32[]{:T(128)}, f32[4480,256]{1,0:T(8,128)}, bf16[8,512,4480]{2,1,0:T(8,128)(2,1)}, bf16[8,512,256]{2,1,0:T(8,128)(2,1)}, s32[]{:T(128)}, ...), condition=%wide.region_20.22_spmd.clone, body=%wide.region_19.21_spmd.clone.sunk | while | flops 1176698880 | bytes 14026326 | solution.py:56
  646.2 5.8 convolution_add_fusion.7
  652.0 7.3 convolution_add_fusion.7
  659.3 7.3 convolution_add_fusion.7
  666.6 7.3 convolution_add_fusion.7
  673.9 7.3 convolution_add_fusion.7
  681.2 7.3 convolution_add_fusion.7
  688.5 7.3 convolution_add_fusion.7
  695.7 7.3 convolution_add_fusion.7
  703.0 6.0 slice_add_fusion.1
  722.1 5.4 all-to-all-done.3
  729.2 7.2 scatter_fusion
  736.4 5.3 multiply_reduce_fusion.1
  752.3 56.4 %while.67 = (s32[]{:T(128)}, f32[4480,256]{1,0:T(8,128)}, bf16[8,512,4480]{2,1,0:T(8,128)(2,1)}, bf16[8,512,256]{2,1,0:T(8,128)(2,1)}, s32[]{:T(128)}, /*index=5*/s32[]{:T(128)}) while((s32[]{:T(128)}, f32[4480,256]{1,0:T(8,128)}, bf16[8,512,4480]{2,1,0:T(8,128)(2,1)}, bf16[8,512,256]{2,1,0:T(8,128)(2,1)}, s32[]{:T(128)}, ...), condition=%wide.region_24.26_spmd.clone, body=%wide.region_23.25_spmd.clone.sunk | while | flops 1176698880 | bytes 14026326 | solution.py:56
  752.3 5.8 convolution_add_fusion.8
  758.1 7.2 convolution_add_fusion.8
  765.3 7.2 convolution_add_fusion.8
  772.6 7.2 convolution_add_fusion.8
  779.8 7.2 convolution_add_fusion.8
  787.0 7.2 convolution_add_fusion.8
  794.3 7.2 convolution_add_fusion.8
  801.5 7.2 convolution_add_fusion.8
  808.7 6.0 slice_add_fusion
  824.1 5.3 all-to-all-done.4
  829.4 6.6 scatter_fusion.1
  836.1 5.3 multiply_reduce_fusion.2
  847.9 36.4 %all-reduce.8.cloned.1.call-done = f32[2,512,256]{1,0,2:T(2,128)} async-done(((f32[2,512,256]{1,0,2:T(2,128)}), f32[2,512,256]{1,0,2:T(2,128)}) %all-reduce.8.cloned.1.call-update) | async-done | bytes 1048592
  891.5 24.8 %reduce-scatter.13.cloned.1.call-done = f32[32,3]{1,0:T(8,128)} async-done(((f32[256,3]{1,0:T(8,128)}), f32[32,3]{1,0:T(8,128)}) %reduce-scatter.13.cloned.1.call-update) | async-done | bytes 400
  917.1 30.4 %reduce-scatter.15.cloned.1.call-done = f32[32,3]{1,0:T(8,128)} async-done(((f32[256,3]{1,0:T(8,128)}), f32[32,3]{1,0:T(8,128)}) %reduce-scatter.15.cloned.1.call-update) | async-done | bytes 400
  948.3 42.1 %all-reduce.6.cloned.1.call-done = f32[2,512,32]{1,2,0:T(8,128)} async-done(((f32[2,512,32]{1,2,0:T(8,128)}), f32[2,512,32]{1,2,0:T(8,128)}) %all-reduce.6.cloned.1.call-update) | async-done | bytes 131088 | tf_op jit(solution)/shard_map/psum | solution.py:233
  991.9 31.4 %reduce-scatter.11.cloned.1.call-done = f32[32,47]{1,0:T(8,128)} async-done(((f32[256,47]{1,0:T(8,128)}), f32[32,47]{1,0:T(8,128)}) %reduce-scatter.11.cloned.1.call-update) | async-done | bytes 6032 | tf_op jit(solution)/shard_map/reduce_scatter | solution.py:229
  1023.3 30.7 %reduce-scatter.9.cloned.1.call-done = f32[200,32]{0,1:T(8,128)} async-done(((f32[200,256]{0,1:T(8,128)}), f32[200,32]{0,1:T(8,128)}) %reduce-scatter.9.cloned.1.call-update) | async-done | bytes 25616 | tf_op jit(solution)/shard_map/reduce_scatter | solution.py:227
  1053.9 17.4 %all-reduce.2 = (f32[200,32]{0,1:T(8,128)S(1)}, f32[32,47]{1,0:T(8,128)S(1)}, f32[3,32]{1,0:T(4,128)S(1)}, f32[3,32]{1,0:T(4,128)S(1)}) all-reduce(f32[200,32]{0,1:T(8,128)} %reduce-scatter.9.cloned.1.call-done, f32[32,47]{1,0:T(8,128)} %reduce-scatter.11.cloned.1.call-done, ...), channel_id=1, replica_groups=mesh['group'=4,'shard'=8] {'group'}, use_global_device_ids=true, to_apply=%region_28.30 | all-reduce | flops 8096 | bytes 64768 | tf_op jit(solution)/shard_map/psum | solution.py:233
  1077.0 14.1 %psum.63 = f32[]{:T(128)} all-reduce(f32[]{:T(128)S(6)} %add.441), channel_id=1, replica_groups=mesh['group'=4,'shard'=8] {'shard'}, use_global_device_ids=true, to_apply=%region_48.50 | all-reduce | flops 1 | bytes 8 | tf_op jit(solution)/shard_map/psum | solution.py:235
  (301 shorter events, 212.7 us)
Async XLA Ops:
  12.8 354.2 %all-to-all-start = ((bf16[32,12,100]{2,1,0:T(8,128)(2,1)}), bf16[32,12,100]{2,1,0:T(8,128)(2,1)S(1)}, u32[]{:S(2)}, u32[]{:S(2)}) async-start(bf16[32,12,100]{2,1,0:T(8,128)(2,1)} %broadcast_select_fusion.2), calls=%async_computation | async-start | bytes 262144 | tf_op jit(solution)/shard_map/all_to_all | solution.py:64
  21.7 12.8 %copy-start.31 = (s32[384]{0:T(512)}, s32[384]{0:T(512)S(1)}, u32[]{:S(2)}) copy-start(s32[384]{0:T(512)S(1)} %reshape.1326) | copy-start | bytes 4612
  35.6 308.0 %copy-start.26 = (f32[200,32]{0,1:T(8,128)S(1)}, f32[200,32]{0,1:T(8,128)}, u32[]{:S(2)}) copy-start(f32[200,32]{0,1:T(8,128)} %param.43) | copy-start | bytes 76804
  35.6 308.0 %copy-start.49 = (f32[3,32]{1,0:T(4,128)S(1)}, f32[3,32]{1,0:T(4,128)}, u32[]{:S(2)}) copy-start(f32[3,32]{1,0:T(4,128)} %param.47) | copy-start | bytes 1156
  353.1 71.6 %copy-start.42 = (f32[1,256]{1,0:T(1,128)}, f32[1,256]{1,0:T(1,128)S(1)}, u32[]{:S(2)}) copy-start(f32[1,256]{1,0:T(1,128)S(1)} %get-tuple-element.385) | copy-start | bytes 3076
  353.1 150.1 %copy-start.44 = (f32[1,256]{1,0:T(1,128)}, f32[1,256]{1,0:T(1,128)S(1)}, u32[]{:S(2)}) copy-start(f32[1,256]{1,0:T(1,128)S(1)} %get-tuple-element.386) | copy-start | bytes 3076
  421.1 1.5 copy-start.18
  422.6 2.0 copy-start.17
  424.7 2.0 copy-start.4
  424.7 3.2 copy-start.22
  426.6 8.1 copy-start.19
  430.8 22.4 %all-to-all-start.1 = ((bf16[32,12,256]{2,1,0:T(8,128)(2,1)}), bf16[32,12,256]{2,1,0:T(8,128)(2,1)S(1)}, u32[]{:S(2)}, u32[]{:S(2)}) async-start(bf16[32,12,256]{2,1,0:T(8,128)(2,1)} %reshape.1327), calls=%async_computation.1 | async-start | bytes 524288 | tf_op jit(solution)/shard_map/all_to_all | solution.py:64
  501.6 1.6 copy-start.15
  503.2 2.0 copy-start.6
  505.2 10.1 copy-start.28
  505.2 10.7 copy-start.56
  511.8 20.4 %all-to-all-start.2 = ((bf16[32,12,256]{2,1,0:T(8,128)(2,1)}), bf16[32,12,256]{2,1,0:T(8,128)(2,1)S(1)}, u32[]{:S(2)}, u32[]{:S(2)}) async-start(bf16[32,12,256]{2,1,0:T(8,128)(2,1)} %reshape.1330), calls=%async_computation.2 | async-start | bytes 524288 | tf_op jit(solution)/shard_map/all_to_all | solution.py:64
  579.6 2.9 copy-start.10
  582.4 1.7 copy-start.16
  582.5 1.6 copy-start.46
  584.1 2.1 copy-start.8
  584.1 2.7 copy-start.40
  584.1 2.9 copy-start.37
  630.5 5.7 copy-start.38
  630.5 5.7 copy-start.9
  630.5 5.7 copy-start.47
  641.2 3.3 copy-start.3
  712.4 15.1 %all-to-all-start.3 = ((bf16[32,12,256]{2,1,0:T(8,128)(2,1)}), bf16[32,12,256]{2,1,0:T(8,128)(2,1)}, u32[]{:S(2)}, u32[]{:S(2)}) async-start(bf16[32,12,256]{2,1,0:T(8,128)(2,1)} %reshape.1334), calls=%async_computation.3 | async-start | bytes 524288 | tf_op jit(solution)/shard_map/all_to_all | solution.py:72
  717.1 12.1 %copy-start.32 = (s32[384]{0:T(512)S(1)}, s32[384]{0:T(512)}, u32[]{:S(2)}) copy-start(s32[384]{0:T(512)} %copy-done.31) | copy-start | bytes 4612
  722.1 14.3 %copy-start.45 = (f32[1,256]{1,0:T(1,128)S(1)}, f32[1,256]{1,0:T(1,128)}, u32[]{:S(2)}) copy-start(f32[1,256]{1,0:T(1,128)} %copy-done.44) | copy-start | bytes 3076
  736.4 5.3 copy-start.1
  736.4 5.9 copy-start.7
  747.3 3.3 copy-start.2
  816.4 13.0 %all-to-all-start.4 = ((bf16[32,12,256]{2,1,0:T(8,128)(2,1)}), bf16[32,12,256]{2,1,0:T(8,128)(2,1)S(1)}, u32[]{:S(2)}, u32[]{:S(2)}) async-start(bf16[32,12,256]{2,1,0:T(8,128)(2,1)} %reshape.1336), calls=%async_computation.4 | async-start | bytes 524288 | tf_op jit(solution)/shard_map/all_to_all | solution.py:72
  819.0 65.3 %all-reduce.8.cloned.1.call-start = ((), (), s32[]{:S(2)}) async-start(), calls=%async_computation.14 | async-start | bytes 2097152
  819.1 3.6 copy-start.21
  824.1 12.0 %copy-start.23 = (f32[4096]{0:T(1024)S(1)}, f32[4096]{0:T(1024)}, u32[]{:S(2)}) copy-start(f32[4096]{0:T(1024)} %copy-done.22) | copy-start | bytes 49156
  824.1 12.0 %copy-start.43 = (f32[1,256]{1,0:T(1,128)S(1)}, f32[1,256]{1,0:T(1,128)}, u32[]{:S(2)}) copy-start(f32[1,256]{1,0:T(1,128)} %copy-done.42) | copy-start | bytes 3076
  824.1 92.2 %reduce-scatter.13.cloned.1.call-start = ((), (), s32[]{:S(2)}) async-start(), calls=%async_computation.12 | async-start | bytes 147456
  836.1 5.3 copy-start
  836.1 6.0 copy-start.5
  842.1 5.0 copy-start.55
  842.1 44.1 %copy-start.14 = (bf16[4096,256]{1,0:T(8,128)(2,1)S(1)}, bf16[4096,256]{1,0:T(8,128)(2,1)}, u32[]{:S(2)}) copy-start(bf16[4096,256]{1,0:T(8,128)(2,1)} %copy-done.13) | copy-start | bytes 6291460
  842.1 44.1 %copy-start.30 = (f32[4096]{0:T(1024)S(1)}, f32[4096]{0:T(1024)}, u32[]{:S(2)}) copy-start(f32[4096]{0:T(1024)} %copy-done.29) | copy-start | bytes 49156
  842.1 44.1 %copy-start.39 = (f32[4096]{0:T(1024)S(1)}, f32[4096]{0:T(1024)}, u32[]{:S(2)}) copy-start(f32[4096]{0:T(1024)} %copy-done.38) | copy-start | bytes 49156
  842.1 44.1 %copy-start.41 = (s32[4096]{0:T(1024)S(1)}, s32[4096]{0:T(1024)}, u32[]{:S(2)}) copy-start(s32[4096]{0:T(1024)} %param.41) | copy-start | bytes 49156
  846.8 100.7 %reduce-scatter.15.cloned.1.call-start = ((), (), s32[]{:S(2)}) async-start(), calls=%async_computation.13 | async-start | bytes 147456
  847.9 142.5 %all-reduce.6.cloned.1.call-start = ((), (), s32[]{:S(2)}) async-start(), calls=%async_computation.10 | async-start | bytes 262144 | tf_op jit(solution)/shard_map/psum | solution.py:233
  885.9 205.9 %copy-start.27 = (f32[200,32]{0,1:T(8,128)S(1)}, f32[200,32]{0,1:T(8,128)}, u32[]{:S(2)}) copy-start(f32[200,32]{0,1:T(8,128)} %param.43) | copy-start | bytes 76804
  885.9 205.9 %copy-start.33 = (f32[200,32]{0,1:T(8,128)S(1)}, f32[200,32]{0,1:T(8,128)}, u32[]{:S(2)}) copy-start(f32[200,32]{0,1:T(8,128)} %param.48) | copy-start | bytes 76804
  886.0 205.9 %copy-start.34 = (f32[200,32]{0,1:T(8,128)S(1)}, f32[200,32]{0,1:T(8,128)}, u32[]{:S(2)}) copy-start(f32[200,32]{0,1:T(8,128)} %param.49) | copy-start | bytes 76804
  886.0 206.5 %copy-start.35 = (f32[32,47]{1,0:T(8,128)S(1)}, f32[32,47]{1,0:T(8,128)}, u32[]{:S(2)}) copy-start(f32[32,47]{1,0:T(8,128)} %param.52) | copy-start | bytes 18052
  886.0 206.5 %copy-start.36 = (f32[32,47]{1,0:T(8,128)S(1)}, f32[32,47]{1,0:T(8,128)}, u32[]{:S(2)}) copy-start(f32[32,47]{1,0:T(8,128)} %param.53) | copy-start | bytes 18052
  886.0 207.2 %copy-start.48 = (f32[3,32]{1,0:T(4,128)S(1)}, f32[3,32]{1,0:T(4,128)}, u32[]{:S(2)}) copy-start(f32[3,32]{1,0:T(4,128)} %param.46) | copy-start | bytes 1156
  886.0 207.2 %copy-start.50 = (f32[3,32]{1,0:T(4,128)S(1)}, f32[3,32]{1,0:T(4,128)}, u32[]{:S(2)}) copy-start(f32[3,32]{1,0:T(4,128)} %param.47) | copy-start | bytes 1156
  886.0 207.1 %copy-start.51 = (f32[3,32]{1,0:T(4,128)S(1)}, f32[3,32]{1,0:T(4,128)}, u32[]{:S(2)}) copy-start(f32[3,32]{1,0:T(4,128)} %param.56) | copy-start | bytes 1156
  886.0 207.1 %copy-start.52 = (f32[3,32]{1,0:T(4,128)S(1)}, f32[3,32]{1,0:T(4,128)}, u32[]{:S(2)}) copy-start(f32[3,32]{1,0:T(4,128)} %param.57) | copy-start | bytes 1156
  886.0 207.1 %copy-start.53 = (f32[3,32]{1,0:T(4,128)S(1)}, f32[3,32]{1,0:T(4,128)}, u32[]{:S(2)}) copy-start(f32[3,32]{1,0:T(4,128)} %param.55) | copy-start | bytes 1156
  886.1 207.1 %copy-start.54 = (f32[3,32]{1,0:T(4,128)S(1)}, f32[3,32]{1,0:T(4,128)}, u32[]{:S(2)}) copy-start(f32[3,32]{1,0:T(4,128)} %param.54) | copy-start | bytes 1156
  886.1 207.7 %copy-start.20 = (f32[2,512,32]{1,2,0:T(8,128)S(1)}, f32[2,512,32]{1,2,0:T(8,128)}, u32[]{:S(2)}) copy-start(f32[2,512,32]{1,2,0:T(8,128)} %param.44) | copy-start | bytes 393220
  886.1 207.7 %copy-start.24 = (f32[2,512,32]{1,2,0:T(8,128)S(1)}, f32[2,512,32]{1,2,0:T(8,128)}, u32[]{:S(2)}) copy-start(f32[2,512,32]{1,2,0:T(8,128)} %param.50) | copy-start | bytes 393220
  886.1 207.7 %copy-start.25 = (f32[2,512,32]{1,2,0:T(8,128)S(1)}, f32[2,512,32]{1,2,0:T(8,128)}, u32[]{:S(2)}) copy-start(f32[2,512,32]{1,2,0:T(8,128)} %param.51) | copy-start | bytes 393220
  886.1 137.2 %reduce-scatter.11.cloned.1.call-start = ((), (), s32[]{:S(2)}) async-start(), calls=%async_computation.11 | async-start | bytes 147456 | tf_op jit(solution)/shard_map/reduce_scatter | solution.py:229
  887.6 166.3 %reduce-scatter.9.cloned.1.call-start = ((), (), s32[]{:S(2)}) async-start(), calls=%async_computation.9 | async-start | bytes 294912 | tf_op jit(solution)/shard_map/reduce_scatter | solution.py:227
  (4 other events, 5.4 us)
Sparse Core Ops, SparseCore 0:
  824.2 60.0 all-reduce.7
  887.1 29.0 reduce-scatter.12
  919.2 28.2 reduce-scatter.14
  950.2 40.0 all-reduce.5
  993.1 30.1 reduce-scatter.10
  1025.4 28.5 reduce-scatter.8
where the time goes:
time: 1110 us; the launch traced here: 1100 us
  other arithmetic  388 us (35%)
  matrix products  258 us (23%)
  waiting for transfers between devices  206 us (19%)
  blocking collectives  140 us (13%)
  local copies, waits for them, and re-layouts  65.6 us (6%)
  between operations  23.1 us (2%)
  starting transfers between devices  22.4 us (2%)
    dynamic_update_slice x8, other arithmetic, build_tables(): return lax.map(build_one_block, (neigh_blocks, degree_blocks))  306 us
    dot_general x24, matrix products, aggregate_one_block(): return jnp.dot(ones_table, table_low, preferred_element_type=jnp.float32)  117 us
    dot_general x16, matrix products, add_block(): lax.dot_general(ones_table, grad_block, (((0,), (0,)), ((), ())), preferr...  113 us
    unnamed x9, waiting for transfers between devices  91.7 us
    psum x1, waiting for transfers between devices, per_device(): lax.psum((split[0], split[1], split[2], split[3], split[4]), 'group')  42.1 us
    psum x1, blocking collectives, per_device(): lax.psum((local_loss, jnp.sum(counted)), ('group', 'shard'))  40.2 us
    reduce_scatter x1, waiting for transfers between devices, per_device(): lax.psum_scatter(local_grads[2], 'shard', scatter_dimension=0, tiled=True)  31.4 us
    reduce_scatter x1, waiting for transfers between devices, per_device(): lax.psum_scatter(local_grads[0], 'shard', scatter_dimension=1, tiled=True)  30.7 us
  transfers between devices with their start and end apart: 11, of which 8 were waited for; matrix products, arithmetic and copies ran while one was open for 32% of the time, Pallas kernels for 0%

commit v1 on v0

v1 whole, which is shorter than its diff:
```python
import functools

import jax
import jax.numpy as jnp
from jax import lax
from jax.experimental import pallas as pl
from jax.experimental.pallas import tpu as pltpu
from jax.sharding import PartitionSpec as P

STEP = 10
MESH = pl.DeviceIdType.MESH
bf16 = jnp.bfloat16
f32 = jnp.float32
i32 = jnp.int32

norm_epsilon = 1e-05
threshold = 0.002
beta_one = 0.5
beta_two = 0.5
adam_epsilon = 1e-08

LANE = 128
LOW = 256
STRIP = 32

NN = (((1,), (0,)), ((), ()))
NT = (((1,), (1,)), ((), ()))
TN = (((0,), (0,)), ((), ()))


def dot(a, b, dims):
    return lax.dot_general(a, b, dims, preferred_element_type=f32)


def round_up(value, unit):
    return -(-value // unit) * unit


def twice(half, width):
    return jnp.concatenate([half] * (width // LANE), axis=1)


def step_kernel(
    cfg,
    feat_ref,
    key_ref,
    deg_ref,
    label_ref,
    mask_ref,
    count_ref,
    send_ref,
    first_ref,
    rest_ref,
    head_ref,
    bias_ref,
    gain_ref,
    grad_out,
    scalar_out,
    counts,
    table1,
    table2,
    table3,
    mean1,
    mean2,
    gmean,
    wide,
    out1,
    in1,
    outs,
    ins,
    info,
    wsend,
    wwire,
    wfull,
    vectors,
    before,
    active,
    slope,
    ghid,
    gacc,
    bacc,
    hacc,
    gfull,
    gwire,
    recv1,
    send2,
    recv2,
    part3,
    recv3,
    scal_send,
    scal_recv,
    row_ssem,
    row_rsem,
    w_ssem,
    w_rsem,
    g_ssem,
    g_rsem,
    s_ssem,
    s_rsem,
):
    n_group, n_shard = cfg["n_group"], cfg["n_shard"]
    nodes, fin, cls = cfg["nodes"], cfg["fin"], cfg["cls"]
    pad, remote, chunk, wire = cfg["pad"], cfg["remote"], cfg["chunk"], cfg["wire"]
    block, fin_pad, hid = cfg["block"], cfg["fin_pad"], cfg["hid"]
    devices = n_group * n_shard
    columns = nodes + remote
    my_group, my_shard = lax.axis_index("group"), lax.axis_index("shard")
    me = my_group * n_shard + my_shard
    blocks = nodes // block

    def target(group, shard):
        return {"group": group, "shard": shard}

    barrier = pltpu.get_barrier_semaphore()

    def greet(i, carry):
        peer = lax.rem(me + i, devices)
        pl.semaphore_signal(
            barrier,
            inc=1,
            device_id=target(lax.div(peer, n_shard), lax.rem(peer, n_shard)),
            device_id_type=MESH,
        )
        return carry

    lax.fori_loop(1, devices, greet, 0)

    def start_rows(source, landing, ssem, rsem):
        def start(i, carry):
            peer = lax.rem(me + i, devices)
            pltpu.make_async_remote_copy(
                src_ref=source.at[pl.ds(pl.multiple_of(peer * pad, pad), pad), :],
                dst_ref=landing.at[pl.ds(pl.multiple_of(me * pad, pad), pad), :],
                send_sem=ssem,
                recv_sem=rsem,
                device_id=target(lax.div(peer, n_shard), lax.rem(peer, n_shard)),
                device_id_type=MESH,
            ).start()
            return carry

        lax.fori_loop(1, devices, start, 0)
        own = pl.ds(pl.multiple_of(me * pad, pad), pad)
        landing[own, :] = source[own, :]

    def wait_bytes(ref, sem):
        pltpu.make_async_copy(ref, ref, sem).wait()

    def wait_rows(source, landing, ssem, rsem):
        rows = pl.ds(0, (devices - 1) * pad)
        wait_bytes(source.at[rows, :], ssem)
        wait_bytes(landing.at[rows, :], rsem)

    some = min(remote, 512)
    row_parts = [slice(r, r + some) for r in range(0, remote, some)]

    def picks(i, rows):
        lanes = lax.broadcasted_iota(i32, (some, LANE), 1) + i * block
        parts = [
            jnp.where(send_ref[rows, :] == lanes + LANE * j, 1.0, 0.0).astype(bf16)
            for j in range(block // LANE)
        ]
        return jnp.concatenate(parts, axis=1)

    def pick_rows(table, into):
        for rows in row_parts:

            def add(i, total):
                off = pl.multiple_of(i * block, block)
                return total + dot(picks(i, rows), table[:, pl.ds(off, block)], NT)

            total = lax.fori_loop(0, blocks, add, jnp.zeros((some, table.shape[0]), f32))
            into[rows, :] = total.astype(bf16)

    total_counted = jnp.zeros((1, LANE), f32)
    lane_row = lax.broadcasted_iota(i32, (1, LANE), 1)
    for r in range(nodes // LANE):
        lanes = slice(r * LANE, (r + 1) * LANE)
        info[0:1, lanes] = 1.0 / deg_ref[r : r + 1, :].astype(f32)
        info[1:2, lanes] = label_ref[r : r + 1, :].astype(f32)
        counted = jnp.where(
            (lane_row + r * LANE < count_ref[0]) & (mask_ref[r : r + 1, :] > 0), 1.0, 0.0
        )
        info[2:3, lanes] = counted
        total_counted = total_counted + counted
    my_count = jnp.sum(total_counted, axis=1, keepdims=True)
    count_high = jnp.floor(my_count * (1.0 / 256.0))
    count_low = my_count - 256.0 * count_high

    table1[...] = jnp.zeros(table1.shape, bf16)
    table1[0:fin, 0:nodes] = feat_ref[...]

    wsend[...] = jnp.zeros(wsend.shape, wire)
    wsend[:, 0:fin] = first_ref[:, 0:fin].astype(bf16).astype(wire)
    wsend[:, LANE : LANE + fin] = first_ref[:, fin : 2 * fin].astype(bf16).astype(wire)
    wsend[:, 2 * LANE : 2 * LANE + cls] = head_ref[...].astype(bf16).astype(wire)
    small = jnp.concatenate(
        [bias_ref[...], gain_ref[...], jnp.zeros((2, chunk), f32)], axis=0
    )
    wsend[:, 3 * LANE : 3 * LANE + 8] = small.T.astype(bf16).astype(wire)
    for level in range(2):
        lanes = slice(4 * LANE + level * 2 * hid, 4 * LANE + (level + 1) * 2 * hid)
        wsend[:, lanes] = rest_ref[level].astype(bf16).astype(wire)

    pick_rows(table1, out1)
    spare = lax.rem(lax.broadcasted_iota(i32, (remote, fin_pad), 0), pad)
    picked = out1[...].astype(f32)
    picked = jnp.where(spare == pad - 2, count_high, picked)
    picked = jnp.where(spare == pad - 1, count_low, picked)
    out1[...] = picked.astype(bf16)

    pl.semaphore_wait(barrier, devices - 1)
    start_rows(out1, in1, row_ssem.at[0], row_rsem.at[0])

    own_chunk = pl.ds(pl.multiple_of(my_shard * chunk, chunk), chunk)

    def send_weights(i, carry):
        shard = lax.rem(my_shard + i, n_shard)
        pltpu.make_async_remote_copy(
            src_ref=wsend,
            dst_ref=wwire.at[own_chunk, :],
            send_sem=w_ssem,
            recv_sem=w_rsem,
            device_id=target(my_group, shard),
            device_id_type=MESH,
        ).start()
        return carry

    lax.fori_loop(1, n_shard, send_weights, 0)
    wwire[own_chunk, :] = wsend[...]

    high_rows = columns // LOW
    low_iota = lax.broadcasted_iota(i32, (LOW, LOW), 0).astype(f32).astype(bf16)
    same_node = (
        lax.div(lax.broadcasted_iota(i32, (16, LOW), 1), 16)
        == lax.broadcasted_iota(i32, (16, LOW), 0)
    ).astype(f32).astype(bf16)
    zero_tile = jnp.zeros((16, LOW), bf16)
    one_low = jnp.ones((LOW, LOW), bf16)
    zero_low = jnp.zeros((LOW, LOW), bf16)
    group_rows = 16 if counts.dtype == bf16 else 32
    fold = group_rows // 16

    def build(it, carry):
        keys = key_ref[pl.ds(pl.multiple_of(it * 8, 8), 8), :]
        high = (keys >> 8).astype(f32)
        low = (keys & 255).astype(f32)
        for k in range(0, 8, fold):
            made = []
            for kk in range(k, k + fold):
                high_row = jnp.broadcast_to(high[kk : kk + 1, :], (16, LOW)).astype(bf16)
                low_row = jnp.broadcast_to(low[kk : kk + 1, :], (16, LOW)).astype(bf16)
                left = jnp.concatenate(
                    [
                        jnp.where(high_row == jnp.asarray(h, bf16), same_node, zero_tile)
                        for h in range(high_rows)
                    ],
                    axis=0,
                )
                right = jnp.where(
                    low_iota == jnp.concatenate([low_row] * (LOW // 16), axis=0),
                    one_low,
                    zero_low,
                )
                made.append(dot(left, right, NT))
            row = pl.multiple_of(it * 128 + k * 16, group_rows)
            for h in range(high_rows):
                tile = jnp.concatenate([m[h * 16 : h * 16 + 16, :] for m in made], axis=0)
                counts[pl.ds(row, group_rows), h * LOW : (h + 1) * LOW] = tile.astype(
                    counts.dtype
                )
        return carry

    lax.fori_loop(0, nodes // 128, build, 0)

    wait_bytes(wwire.at[pl.ds(0, (n_shard - 1) * chunk), :], w_rsem)
    for _ in range(n_shard - 1):
        wait_bytes(wsend, w_ssem)
    wfull[...] = wwire[...].astype(bf16)
    weight_lanes = (
        slice(0, 2 * LANE),
        slice(4 * LANE, 4 * LANE + 2 * hid),
        slice(4 * LANE + 2 * hid, 4 * LANE + 4 * hid),
    )
    small_full = wfull[:, 3 * LANE : 4 * LANE].astype(f32)
    for v in range(6):
        vectors[v] = jnp.broadcast_to(small_full[:, v : v + 1], (hid, LANE))

    def matrix(level):
        return wfull[:, weight_lanes[level]]

    wait_rows(out1, in1, row_ssem.at[0], row_rsem.at[0])
    received = in1[...].astype(f32)
    scale = jnp.where(spare == pad - 2, 256.0, jnp.where(spare == pad - 1, 1.0, 0.0))
    label_count = jnp.sum(received * scale, axis=0, keepdims=True)
    table1[:, nodes:] = in1[...].T

    def c_block(off, lanes):
        return counts[pl.ds(off, block), lanes].astype(bf16)

    strips = [slice(r, r + STRIP) for r in range(0, hid, STRIP)]

    def fold_rows(value):
        return jnp.sum(value.reshape(STRIP // 8, 8, value.shape[1]), axis=0)

    def activate(level, keep_slope, store_before):
        squares = jnp.zeros((8, block), f32)
        for st in strips:
            b = before[st, :] + twice(vectors[level, st, :], block)
            s = 0.5 + 0.5 * jnp.tanh(0.5 * b)
            a = b * s
            active[st, :] = a
            if keep_slope:
                slope[st, :] = s + a * (1.0 - s)
            squares = squares + fold_rows(a * a)
        mean_square = jnp.sum(squares, axis=0, keepdims=True) * (1.0 / hid)
        return lax.rsqrt(mean_square + norm_epsilon)

    def hidden_strip(level, st, inverse):
        return (twice(vectors[3 + level, st, :], block) * (active[st, :] * inverse)).astype(bf16)

    def forward_block(level, off, summed, table, mean, keep_slope):
        lanes = pl.ds(off, block)
        mean_low = (summed * info[0:1, lanes]).astype(bf16)
        if mean is not None:
            mean[:, lanes] = mean_low
        joined = jnp.concatenate([table[:, lanes], mean_low], axis=0)
        before[...] = dot(matrix(level), joined, NN)
        return joined, activate(level, keep_slope, False)

    def layer_one(i, carry):
        off = pl.multiple_of(i * block, block)
        summed = dot(table1[...], c_block(off, slice(0, columns)), NT)
        _, inverse = forward_block(0, off, summed, table1, mean1, False)
        for st in strips:
            table2[st, pl.ds(off, block)] = hidden_strip(0, st, inverse)
        return carry

    lax.fori_loop(0, blocks, layer_one, 0)

    def own_sums(table):
        def add(i, carry):
            off = pl.multiple_of(i * block, block)
            wide[:, pl.ds(off, block)] = dot(
                table[:, 0:nodes], c_block(off, slice(0, nodes)), NT
            )
            return carry

        lax.fori_loop(0, blocks, add, 0)

    def exchange_forward(table, x):
        pick_rows(table, outs)
        start_rows(outs, ins.at[x], row_ssem.at[x + 1], row_rsem.at[x + 1])
        own_sums(table)
        wait_rows(outs, ins.at[x], row_ssem.at[x + 1], row_rsem.at[x + 1])
        table[:, nodes:] = ins[x].T

    def all_sums(table, off):
        return wide[:, pl.ds(off, block)] + dot(
            table[:, nodes:], c_block(off, slice(nodes, columns)), NT
        )

    exchange_forward(table2, 0)

    def layer_two(i, carry):
        off = pl.multiple_of(i * block, block)
        _, inverse = forward_block(1, off, all_sums(table2, off), table2, mean2, False)
        for st in strips:
            table3[st, pl.ds(off, block)] = hidden_strip(1, st, inverse)
        return carry

    lax.fori_loop(0, blocks, layer_two, 0)

    exchange_forward(table3, 1)
    gfull[...] = jnp.zeros(gfull.shape, f32)
    gacc[...] = jnp.zeros(gacc.shape, f32)
    bacc[...] = jnp.zeros(bacc.shape, f32)
    head_low = wfull[:, 2 * LANE : 3 * LANE]
    cls_pad = round_up(cls, 16)
    one_over_count = 1.0 / label_count[0:1, 0:1]
    class_iota = lax.broadcasted_iota(i32, (cls_pad, block), 0)

    def backward_block(level, off, joined, inverse, need_input):
        lanes = pl.ds(off, block)
        crossed = jnp.zeros((8, block), f32)
        for st in strips:
            u = ghid[st, :] * twice(vectors[3 + level, st, :], block)
            crossed = crossed + fold_rows(u * active[st, :])
        factor = jnp.sum(crossed, axis=0, keepdims=True) * (1.0 / hid) * inverse
        factor = factor * inverse * inverse
        low_parts = []
        for st in strips:
            g = ghid[st, :]
            a = active[st, :]
            u = g * twice(vectors[3 + level, st, :], block)
            low = ((inverse * u - a * factor) * slope[st, :]).astype(bf16)
            low_parts.append(low)
            gain_term = g * (a * inverse)
            bias_term = low.astype(f32)
            gain_sum = gain_term[:, 0:LANE]
            bias_sum = bias_term[:, 0:LANE]
            for j in range(1, block // LANE):
                gain_sum = gain_sum + gain_term[:, j * LANE : (j + 1) * LANE]
                bias_sum = bias_sum + bias_term[:, j * LANE : (j + 1) * LANE]
            gacc[level, st, :] += gain_sum
            bacc[level, st, :] += bias_sum
        low = jnp.concatenate(low_parts, axis=0)
        seg = (0, 1, 2)[level]
        pieces = joined.shape[0] // LANE
        added = dot(low, joined, NT)
        for j in range(pieces):
            gfull[seg, j] += added[:, j * LANE : (j + 1) * LANE]
        if need_input:
            back = dot(matrix(level), low, TN)
            wide[:, lanes] = back[0:hid, :]
            gmean[:, lanes] = (back[hid:, :] * info[0:1, lanes]).astype(bf16)

    def layer_three(i, loss):
        off = pl.multiple_of(i * block, block)
        lanes = pl.ds(off, block)
        joined, inverse = forward_block(2, off, all_sums(table3, off), table3, None, True)
        last = jnp.concatenate([hidden_strip(2, st, inverse) for st in strips], axis=0)
        logits = dot(head_low, last, TN)[0:cls_pad, :]
        logits = jnp.where(class_iota < cls, logits, -jnp.inf)
        highest = jnp.max(logits, axis=0, keepdims=True)
        shifted = logits - highest
        grown = jnp.exp(shifted)
        total = jnp.sum(grown, axis=0, keepdims=True)
        hot = class_iota == info[1:2, lanes].astype(i32)
        counted = info[2:3, lanes]
        chosen = jnp.sum(jnp.where(hot, shifted, 0.0), axis=0, keepdims=True)
        loss = loss + (jnp.log(total) - chosen) * counted
        g_logits = (grown / total - jnp.where(hot, 1.0, 0.0)) * (counted * one_over_count)
        g_low = jnp.concatenate(
            [g_logits, jnp.zeros((LANE - cls_pad, block), f32)], axis=0
        ).astype(bf16)
        gfull[0, 2] += dot(last, g_low, NT)
        ghid[...] = dot(head_low, g_low, NN)
        backward_block(2, off, joined, inverse, True)
        return loss

    loss = lax.fori_loop(0, blocks, layer_three, jnp.zeros((1, block), f32))

    def start_first(seg):
        for piece in range(n_group):
            gwire[seg, piece] = gfull[seg, piece].astype(wire)

        def start(i, carry):
            group = lax.rem(my_group + i, n_group)
            pltpu.make_async_remote_copy(
                src_ref=gwire.at[seg, group],
                dst_ref=recv1.at[seg, my_group],
                send_sem=g_ssem.at[0, seg],
                recv_sem=g_rsem.at[0, seg],
                device_id=target(group, my_shard),
                device_id_type=MESH,
            ).start()
            return carry

        lax.fori_loop(1, n_group, start, 0)
        recv1[seg, my_group] = jnp.zeros(recv1.shape[2:], wire)

    def start_second(seg):
        wait_bytes(gwire.at[seg, pl.ds(0, n_group - 1)], g_ssem.at[0, seg])
        wait_bytes(recv1.at[seg, pl.ds(0, n_group - 1)], g_rsem.at[0, seg])
        total = gfull[seg, my_group]
        for group in range(n_group):
            total = total + recv1[seg, group].astype(f32)
        gfull[seg, my_group] = total
        send2[seg] = total.astype(wire).reshape(n_shard, chunk, LANE)

        def start(i, carry):
            shard = lax.rem(my_shard + i, n_shard)
            pltpu.make_async_remote_copy(
                src_ref=send2.at[seg, shard],
                dst_ref=recv2.at[seg, my_shard],
                send_sem=g_ssem.at[1, seg],
                recv_sem=g_rsem.at[1, seg],
                device_id=target(my_group, shard),
                device_id_type=MESH,
            ).start()
            return carry

        lax.fori_loop(1, n_shard, start, 0)
        recv2[seg, my_shard] = jnp.zeros(recv2.shape[2:], wire)

    def start_third(seg):
        wait_bytes(send2.at[seg, pl.ds(0, n_shard - 1)], g_ssem.at[1, seg])
        wait_bytes(recv2.at[seg, pl.ds(0, n_shard - 1)], g_rsem.at[1, seg])
        total = gfull[seg, my_group, own_chunk, :]
        for shard in range(n_shard):
            total = total + recv2[seg, shard].astype(f32)
        part3[seg] = total

        def start(i, carry):
            group = lax.rem(my_group + i, n_group)
            pltpu.make_async_remote_copy(
                src_ref=part3.at[seg],
                dst_ref=recv3.at[seg, my_group],
                send_sem=g_ssem.at[2, seg],
                recv_sem=g_rsem.at[2, seg],
                device_id=target(group, my_shard),
                device_id_type=MESH,
            ).start()
            return carry

        lax.fori_loop(1, n_group, start, 0)
        recv3[seg, my_group] = total
        return jnp.sum(total * total)

    def wait_third(seg):
        for _ in range(n_group - 1):
            wait_bytes(part3.at[seg], g_ssem.at[2, seg])
        wait_bytes(recv3.at[seg, pl.ds(0, n_group - 1)], g_rsem.at[2, seg])

    def exchange_backward(x):
        for rows in row_parts:
            lanes = slice(nodes + rows.start, nodes + rows.stop)
            back = dot(gmean[...], counts[:, lanes].astype(bf16), NN)
            outs[rows, :] = back.astype(bf16).T
        start_rows(outs, ins.at[x], row_ssem.at[x + 1], row_rsem.at[x + 1])

        def add(i, carry):
            off = pl.multiple_of(i * block, block)
            lanes = pl.ds(off, block)
            wide[:, lanes] += dot(gmean[...], counts[:, lanes].astype(bf16), NN)
            return carry

        lax.fori_loop(0, blocks, add, 0)
        wait_rows(outs, ins.at[x], row_ssem.at[x + 1], row_rsem.at[x + 1])

    def returned(x, i):
        off = pl.multiple_of(i * block, block)
        total = wide[:, pl.ds(off, block)]
        for rows in row_parts:
            total = total + dot(ins[x, rows, :], picks(i, rows), TN)
        return total

    start_first(2)
    exchange_backward(2)
    start_second(2)

    def backward_two(i, carry):
        off = pl.multiple_of(i * block, block)
        lanes = pl.ds(off, block)
        ghid[...] = returned(2, i)
        joined = jnp.concatenate([table2[:, lanes], mean2[:, lanes]], axis=0)
        before[...] = dot(matrix(1), joined, NN)
        inverse = activate(1, True, False)
        backward_block(1, off, joined, inverse, True)
        return carry

    lax.fori_loop(0, blocks, backward_two, 0)
    start_first(1)
    square = start_third(2)
    exchange_backward(3)
    start_second(1)

    def backward_one(i, carry):
        off = pl.multiple_of(i * block, block)
        lanes = pl.ds(off, block)
        ghid[...] = returned(3, i)
        joined = jnp.concatenate([table1[:, lanes], mean1[:, lanes]], axis=0)
        before[...] = dot(matrix(0), joined, NN)
        inverse = activate(0, True, False)
        backward_block(0, off, joined, inverse, False)
        return carry

    lax.fori_loop(0, blocks, backward_one, 0)
    lane_wide = lax.broadcasted_iota(i32, (hid, LANE), 1)
    small_grad = jnp.zeros((hid, LANE), f32)
    for level in range(3):
        small_grad = jnp.where(
            lane_wide == level, jnp.sum(bacc[level], axis=1, keepdims=True), small_grad
        )
        small_grad = jnp.where(
            lane_wide == 3 + level, jnp.sum(gacc[level], axis=1, keepdims=True), small_grad
        )
    gfull[0, 3] = small_grad
    start_first(0)
    square = square + start_third(1)
    start_second(0)
    square = square + start_third(0)

    row8 = lax.broadcasted_iota(i32, (8, LANE), 0)
    mine = jnp.where(row8 == 0, square, jnp.where(row8 == 1, jnp.sum(loss), 0.0))
    scal_send[...] = mine

    def send_scalars(i, carry):
        peer = lax.rem(me + i, devices)
        pltpu.make_async_remote_copy(
            src_ref=scal_send,
            dst_ref=scal_recv.at[me],
            send_sem=s_ssem,
            recv_sem=s_rsem,
            device_id=target(lax.div(peer, n_shard), lax.rem(peer, n_shard)),
            device_id_type=MESH,
        ).start()
        return carry

    lax.fori_loop(1, devices, send_scalars, 0)
    scal_recv[me] = mine
    for seg in range(3):
        wait_third(seg)
    grad_out[...] = recv3[...]
    wait_bytes(scal_recv.at[pl.ds(0, devices - 1)], s_rsem)

    def drain(i, carry):
        wait_bytes(scal_send, s_ssem)
        return carry

    lax.fori_loop(1, devices, drain, 0)
    scalar_out[...] = jnp.where(
        row8 == 2, label_count[0:1, 0:1], jnp.sum(scal_recv[...], axis=0)
    )


def adamw(weight, grad, moment, square, rate, decay):
    moment_new = beta_one * moment + (1.0 - beta_one) * grad
    square_new = beta_two * square + (1.0 - beta_two) * grad * grad
    moment_hat = moment_new / (1.0 - beta_one**STEP)
    square_hat = square_new / (1.0 - beta_two**STEP)
    weight_new = weight - rate * (
        moment_hat / (jnp.sqrt(square_hat) + adam_epsilon) + decay * weight
    )
    return (weight_new, moment_new, square_new)


def per_device(
    n_group,
    n_shard,
    features,
    node_counts,
    degrees,
    neighbours,
    send_rows,
    labels,
    train_mask,
    weight_first,
    weight_rest,
    weight_head,
    biases,
    gains,
    moment_first,
    square_first,
    moment_rest,
    square_rest,
    moment_head,
    square_head,
    moment_bias,
    square_bias,
    moment_gain,
    square_gain,
):
    nodes, fin = features.shape
    devices = n_group * n_shard
    hid = weight_rest.shape[1] // 2
    chunk = hid // n_shard
    cls = weight_head.shape[1]
    cap = send_rows.shape[1]
    slots = neighbours.shape[1]
    pad = round_up(cap + 2, 16)
    remote = devices * pad
    columns = nodes + remote
    block = 256
    wire = bf16 if chunk % 16 == 0 else f32
    counts_dtype = bf16 if nodes * columns * 2 <= 40 * 2**20 else jnp.float8_e4m3fn
    fin_pad = LANE
    cfg = dict(
        n_group=n_group,
        n_shard=n_shard,
        nodes=nodes,
        fin=fin,
        cls=cls,
        pad=pad,
        remote=remote,
        chunk=chunk,
        wire=wire,
        block=block,
        fin_pad=fin_pad,
        hid=hid,
    )

    away = neighbours - nodes
    source = away // cap
    moved = nodes + source * pad + (away - source * cap)
    mapped = jnp.where(away < 0, neighbours, moved)
    live = lax.broadcasted_iota(i32, mapped.shape, 1) < degrees[:, None]
    keys = jnp.where(live, mapped, -1).reshape(nodes // 16, 16 * slots)
    send_padded = jnp.pad(send_rows, ((0, 0), (0, pad - cap)), constant_values=-1)
    send_wide = jnp.broadcast_to(send_padded.reshape(remote, 1), (remote, LANE))

    vmem = pl.BlockSpec(memory_space=pltpu.VMEM)
    smem = pl.BlockSpec(memory_space=pltpu.SMEM)
    width = 4 * LANE + 4 * hid
    dma = pltpu.SemaphoreType.DMA
    scratch = [
        pltpu.VMEM((nodes, columns), counts_dtype),
        pltpu.VMEM((fin_pad, columns), bf16),
        pltpu.VMEM((hid, columns), bf16),
        pltpu.VMEM((hid, columns), bf16),
        pltpu.VMEM((fin_pad, nodes), bf16),
        pltpu.VMEM((hid, nodes), bf16),
        pltpu.VMEM((hid, nodes), bf16),
        pltpu.VMEM((hid, nodes), f32),
        pltpu.VMEM((remote, fin_pad), bf16),
        pltpu.VMEM((remote, fin_pad), bf16),
        pltpu.VMEM((remote, hid), bf16),
        pltpu.VMEM((4, remote, hid), bf16),
        pltpu.VMEM((8, nodes), f32),
        pltpu.VMEM((chunk, width), wire),
        pltpu.VMEM((hid, width), wire),
        pltpu.VMEM((hid, width), bf16),
        pltpu.VMEM((6, hid, LANE), f32),
        pltpu.VMEM((hid, block), f32),
        pltpu.VMEM((hid, block), f32),
        pltpu.VMEM((hid, block), f32),
        pltpu.VMEM((hid, block), f32),
        pltpu.VMEM((3, hid, LANE), f32),
        pltpu.VMEM((3, hid, LANE), f32),
        pltpu.VMEM((8, LANE), f32),
        pltpu.VMEM((3, n_group, hid, LANE), f32),
        pltpu.VMEM((3, n_group, hid, LANE), wire),
        pltpu.VMEM((3, n_group, hid, LANE), wire),
        pltpu.VMEM((3, n_shard, chunk, LANE), wire),
        pltpu.VMEM((3, n_shard, chunk, LANE), wire),
        pltpu.VMEM((3, chunk, LANE), f32),
        pltpu.VMEM((3, n_group, chunk, LANE), f32),
        pltpu.VMEM((8, LANE), f32),
        pltpu.VMEM((devices, 8, LANE), f32),
        dma((5,)),
        dma((5,)),
        dma,
        dma,
        dma((3, 3)),
        dma((3, 3)),
        dma,
        dma,
    ]
    grads, scalars = pl.pallas_call(
        functools.partial(step_kernel, cfg),
        out_shape=(
            jax.ShapeDtypeStruct((3, n_group, chunk, LANE), f32),
            jax.ShapeDtypeStruct((8, LANE), f32),
        ),
        in_specs=[vmem] * 5 + [smem] + [vmem] * 6,
        out_specs=(vmem, vmem),
        scratch_shapes=scratch,
        compiler_params=pltpu.CompilerParams(
            collective_id=0, has_side_effects=True, vmem_limit_bytes=63 * 2**20
        ),
    )(
        features.T,
        keys,
        degrees.reshape(nodes // LANE, LANE),
        labels.reshape(nodes // LANE, LANE),
        train_mask.reshape(nodes // LANE, LANE),
        node_counts,
        send_wide,
        weight_first.T,
        weight_rest.transpose(0, 2, 1),
        weight_head,
        biases,
        gains,
    )
    grad_norm = jnp.sqrt(scalars[0, 0])
    loss_sum = scalars[1, 0]
    label_count = scalars[2, 0]
    factor = jnp.minimum(1.0, threshold / grad_norm)
    grads = grads * factor
    grad_first = jnp.concatenate([grads[0, 0, :, :fin], grads[0, 1, :, :fin]], axis=1).T
    grad_rest = jnp.stack(
        [jnp.concatenate([grads[s, j] for j in range(n_group)], axis=1).T for s in (1, 2)]
    )
    grad_head = grads[0, 2, :, :cls]
    grad_bias = grads[0, 3, :, 0:3].T
    grad_gain = grads[0, 3, :, 3:6].T
    first_out = adamw(weight_first, grad_first, moment_first, square_first, 0.05, 0.01)
    rest_out = adamw(weight_rest, grad_rest, moment_rest, square_rest, 0.05, 0.01)
    head_out = adamw(weight_head, grad_head, moment_head, square_head, 0.05, 0.01)
    bias_out = adamw(biases, grad_bias, moment_bias, square_bias, 0.3, 0.0)
    gain_out = adamw(gains, grad_gain, moment_gain, square_gain, 0.3, 0.0)
    return (
        (loss_sum, label_count, grad_norm)
        + first_out
        + rest_out
        + head_out
        + bias_out
        + gain_out
        + (first_out[0].astype(bf16), rest_out[0].astype(bf16), head_out[0].astype(bf16))
    )


def solution(mesh):
    nodes_split = P(("group", "shard"))
    nodes_rows = P(("group", "shard"), None)
    first = P(None, "shard")
    rest = P(None, None, "shard")
    head = P("shard", None)
    return jax.shard_map(
        functools.partial(per_device, mesh.shape["group"], mesh.shape["shard"]),
        mesh=mesh,
        in_specs=(
            nodes_rows,
            nodes_split,
            nodes_split,
            nodes_rows,
            nodes_rows,
            nodes_split,
            nodes_split,
            first,
            rest,
            head,
            first,
            first,
            first,
            first,
            rest,
            rest,
            head,
            head,
            first,
            first,
            first,
            first,
        ),
        out_specs=(P(), P(), P())
        + (first,) * 3
        + (rest,) * 3
        + (head,) * 3
        + (first,) * 6
        + (first, rest, head),
        check_vma=False,
    )
```

time: 1110 us -> 193 us (0.17)
  other arithmetic: 388 us -> 4.95 us
  matrix products: 258 us -> 0 us
  waiting for transfers between devices: 206 us -> 0 us
  Pallas kernels: 0 us -> 180 us
  blocking collectives: 140 us -> 0 us
  local copies, waits for them, and re-layouts: 65.6 us -> 4.79 us
  starting transfers between devices: 22.4 us -> 0 us
  between operations: 23.1 us -> 3.39 us
    dynamic_update_slice x8 -> x0, other arithmetic: 306 us -> none  [build_tables(): return lax.map(build_one_block, (neigh_blocks, degree_blocks))]
    dot_general x51 -> x0, matrix products: 258 us -> none  [the longest x24 117 us: aggregate_one_block(): return jnp.dot(ones_table, table_low, preferred_element_type=jnp.float32)]
    pallas_call x0 -> x1, Pallas kernels: none -> 180 us  [per_device(): pl.pallas_call(functools.partial(step_kernel, cfg), out_shape=(jax.ShapeD...]
    unnamed x9 -> x0, waiting for transfers between devices: 91.7 us -> none
    psum x3 -> x0, blocking collectives: 71.7 us -> none  [the longest x1 40.2 us: per_device(): lax.psum((local_loss, jnp.sum(counted)), ('group', 'shard'))]
    all_gather x5 -> x0, blocking collectives: 68.1 us -> none  [the longest x1 18.4 us: per_device(): lax.all_gather(weight_rest.astype(jnp.bfloat16), 'shard', axis=2, tiled=T...]
    reduce_scatter x2 -> x0, waiting for transfers between devices: 62.1 us -> none  [the longest x1 31.4 us: per_device(): lax.psum_scatter(local_grads[2], 'shard', scatter_dimension=0, tiled=True)]
    psum x1 -> x0, waiting for transfers between devices: 42.1 us -> none  [per_device(): lax.psum((split[0], split[1], split[2], split[3], split[4]), 'group')]
  transfers between devices with their start and end apart: 11 -> 0, of which waited for: 8 -> 0; matrix products, arithmetic and copies ran while one was open for 32% -> 0% of each run, Pallas kernels for 0% -> 0%
where the time goes in v1:
time: 193 us
  Pallas kernels  180 us (93%)
  other arithmetic  4.95 us (3%)
  local copies, waits for them, and re-layouts  4.79 us (2%)
  between operations  3.39 us (2%)
    pallas_call x1, Pallas kernels, per_device(): pl.pallas_call(functools.partial(step_kernel, cfg), out_shape=(jax.ShapeD...  180 us

profile of v1, /device:TPU:0, one launch (start us, length us, event | category | flops | bytes accessed | tf_op | source)
XLA Modules:
  0.0 192.8 jit_solution(810935763910752056)
XLA Ops:
  0.7 1.2 select_select_fusion
  1.9 0.0 copy-start.11
  1.9 0.6 copy.46
  2.5 0.0 copy-start
  2.5 0.0 copy-start.1
  2.5 0.0 copy-start.2
  2.5 1.5 reshape.58.key_ref
  4.1 0.0 copy-done.11
  4.1 0.0 copy-start.9
  4.1 0.0 copy-start.10
  4.1 0.0 copy-start.12
  4.1 0.0 copy-start.13
  4.1 0.0 copy-start.14
  4.1 0.0 copy-start.15
  4.1 0.0 copy-start.3
  4.1 0.0 copy-start.5
  4.1 0.0 copy-start.6
  4.1 0.1 copy.50
  4.2 0.1 broadcast_in_dim.10
  4.3 0.0 copy-start.4
  4.3 0.0 copy-start.7
  4.3 0.0 copy-start.8
  4.3 0.8 broadcast_in_dim.11.send_ref
  5.8 179.7 %shard_map.373 = (f32[3,4,32,128]{3,2,1,0:T(8,128)}, f32[8,128]{1,0:T(8,128)}) custom-call(bf16[100,4096]{1,0:T(8,128)(2,1)} %bitcast.67, s32[256,256]{1,0:T(8,128)} %reshape.58.key_ref, s32[32,128]{1,0:T(8,128)} %bitcast.70, s32[32,128]{1,0:T(8,128)} %bitcast.71, s32[32,128]{1,0:T(8,128)} %bitcast.72, s32[1]{0:T(128)S(6)} %copy.51.count_ref, ...), custom_call_target="tpu_custom_call" | custom-call | tf_op jit(solution)/shard_map/pallas_call | solution.py:739
  185.5 1.3 fusion.17
  187.6 0.9 broadcast_multiply_fusion
  188.5 0.0 copy-done
  188.6 0.0 copy-done.1
  188.6 0.0 copy-done.2
  188.6 0.8 fusion.10
  189.4 0.1 fusion.16
  189.5 0.1 copy.48
  189.5 0.1 copy.49
  189.6 0.0 copy-done.9
  189.6 0.0 copy-done.10
  189.6 0.0 copy-done.12
  189.6 0.0 copy-done.13
  189.6 0.0 copy-done.14
  189.7 0.0 copy-done.15
  189.7 0.6 multiply_subtract_fusion.3
  190.3 0.0 copy-done.3
  190.3 0.0 copy-done.5
  190.3 0.0 copy-done.6
  190.3 0.7 fusion.12
  191.0 0.0 copy-done.4
  191.0 0.0 copy-done.7
  191.0 0.0 copy-done.8
  191.0 0.6 fusion.8
  (4 shorter events, 0.0 us)
Async XLA Ops:
  1.9 2.2 %copy-start.11 = (s32[32,12]{0,1:T(8,128)S(1)}, s32[32,12]{0,1:T(8,128)}, u32[]{:S(2)}) copy-start(s32[32,12]{0,1:T(8,128)} %param.26) | copy-start | bytes 4612
  2.5 186.1 %copy-start = (f32[2,512,32]{1,2,0:T(8,128)S(1)}, f32[2,512,32]{1,2,0:T(8,128)}, u32[]{:S(2)}) copy-start(f32[2,512,32]{1,2,0:T(8,128)} %param.30) | copy-start | bytes 393220
  2.5 186.1 %copy-start.1 = (f32[2,512,32]{1,2,0:T(8,128)S(1)}, f32[2,512,32]{1,2,0:T(8,128)}, u32[]{:S(2)}) copy-start(f32[2,512,32]{1,2,0:T(8,128)} %param.36) | copy-start | bytes 393220
  2.5 186.1 %copy-start.2 = (f32[2,512,32]{1,2,0:T(8,128)S(1)}, f32[2,512,32]{1,2,0:T(8,128)}, u32[]{:S(2)}) copy-start(f32[2,512,32]{1,2,0:T(8,128)} %param.37) | copy-start | bytes 393220
  4.1 185.6 %copy-start.9 = (f32[3,32]{1,0:T(4,128)S(1)}, f32[3,32]{1,0:T(4,128)}, u32[]{:S(2)}) copy-start(f32[3,32]{1,0:T(4,128)} %bias_ref.1) | copy-start | bytes 1156
  4.1 185.6 %copy-start.10 = (f32[3,32]{1,0:T(4,128)S(1)}, f32[3,32]{1,0:T(4,128)}, u32[]{:S(2)}) copy-start(f32[3,32]{1,0:T(4,128)} %gain_ref.1) | copy-start | bytes 1156
  4.1 185.6 %copy-start.12 = (f32[3,32]{1,0:T(4,128)S(1)}, f32[3,32]{1,0:T(4,128)}, u32[]{:S(2)}) copy-start(f32[3,32]{1,0:T(4,128)} %param.42) | copy-start | bytes 1156
  4.1 185.6 %copy-start.13 = (f32[3,32]{1,0:T(4,128)S(1)}, f32[3,32]{1,0:T(4,128)}, u32[]{:S(2)}) copy-start(f32[3,32]{1,0:T(4,128)} %param.43) | copy-start | bytes 1156
  4.1 185.6 %copy-start.14 = (f32[3,32]{1,0:T(4,128)S(1)}, f32[3,32]{1,0:T(4,128)}, u32[]{:S(2)}) copy-start(f32[3,32]{1,0:T(4,128)} %param.41) | copy-start | bytes 1156
  4.1 185.6 %copy-start.15 = (f32[3,32]{1,0:T(4,128)S(1)}, f32[3,32]{1,0:T(4,128)}, u32[]{:S(2)}) copy-start(f32[3,32]{1,0:T(4,128)} %param.40) | copy-start | bytes 1156
  4.1 186.2 %copy-start.3 = (f32[200,32]{0,1:T(8,128)S(1)}, f32[200,32]{0,1:T(8,128)}, u32[]{:S(2)}) copy-start(f32[200,32]{0,1:T(8,128)} %param.29) | copy-start | bytes 76804
  4.1 186.2 %copy-start.5 = (f32[200,32]{0,1:T(8,128)S(1)}, f32[200,32]{0,1:T(8,128)}, u32[]{:S(2)}) copy-start(f32[200,32]{0,1:T(8,128)} %param.34) | copy-start | bytes 76804
  4.1 186.2 %copy-start.6 = (f32[200,32]{0,1:T(8,128)S(1)}, f32[200,32]{0,1:T(8,128)}, u32[]{:S(2)}) copy-start(f32[200,32]{0,1:T(8,128)} %param.35) | copy-start | bytes 76804
  4.3 186.7 %copy-start.4 = (f32[32,47]{1,0:T(8,128)S(1)}, f32[32,47]{1,0:T(8,128)}, u32[]{:S(2)}) copy-start(f32[32,47]{1,0:T(8,128)} %head_ref.1) | copy-start | bytes 18052
  4.3 186.7 %copy-start.7 = (f32[32,47]{1,0:T(8,128)S(1)}, f32[32,47]{1,0:T(8,128)}, u32[]{:S(2)}) copy-start(f32[32,47]{1,0:T(8,128)} %param.38) | copy-start | bytes 18052
  4.3 186.7 %copy-start.8 = (f32[32,47]{1,0:T(8,128)S(1)}, f32[32,47]{1,0:T(8,128)}, u32[]{:S(2)}) copy-start(f32[32,47]{1,0:T(8,128)} %param.39) | copy-start | bytes 18052

commit v2 on v1

--- a/solution.py
+++ b/solution.py
@@ -21,6 +21,7 @@
 
 LANE = 128
 LOW = 256
+narrow = jnp.float8_e4m3fn
 STRIP = 32
 
 NN = (((1,), (0,)), ((), ()))
@@ -54,14 +55,21 @@
     head_ref,
     bias_ref,
     gain_ref,
-    grad_out,
+    part_out,
+    head_out,
+    first_out,
     scalar_out,
     counts,
+    picked,
     table1,
     table2,
     table3,
+    first_own,
+    first_remote,
     mean1,
     mean2,
+    before1,
+    before2,
     gmean,
     wide,
     out1,
@@ -79,7 +87,6 @@
     ghid,
     gacc,
     bacc,
-    hacc,
     gfull,
     gwire,
     recv1,
@@ -87,6 +94,16 @@
     recv2,
     part3,
     recv3,
+    gfirst,
+    fwire,
+    frecv,
+    fpart,
+    ffinal,
+    ghead,
+    hwire,
+    hrecv,
+    hpart,
+    hfinal,
     scal_send,
     scal_recv,
     row_ssem,
@@ -95,6 +112,10 @@
     w_rsem,
     g_ssem,
     g_rsem,
+    f_ssem,
+    f_rsem,
+    h_ssem,
+    h_rsem,
     s_ssem,
     s_rsem,
 ):
@@ -153,22 +174,30 @@
     some = min(remote, 512)
     row_parts = [slice(r, r + some) for r in range(0, remote, some)]
 
-    def picks(i, rows):
-        lanes = lax.broadcasted_iota(i32, (some, LANE), 1) + i * block
+    def make_picks(rows, off, width):
+        lanes = lax.broadcasted_iota(i32, (some, LANE), 1) + off
         parts = [
             jnp.where(send_ref[rows, :] == lanes + LANE * j, 1.0, 0.0).astype(bf16)
-            for j in range(block // LANE)
+            for j in range(width // LANE)
         ]
         return jnp.concatenate(parts, axis=1)
 
+    def picks(rows, off):
+        if picked.shape[0] == remote:
+            return picked[rows, pl.ds(off, block)].astype(bf16)
+        return make_picks(rows, off, block)
+
     def pick_rows(table, into):
         for rows in row_parts:
-
-            def add(i, total):
-                off = pl.multiple_of(i * block, block)
-                return total + dot(picks(i, rows), table[:, pl.ds(off, block)], NT)
-
-            total = lax.fori_loop(0, blocks, add, jnp.zeros((some, table.shape[0]), f32))
+            if picked.shape[0] == remote:
+                total = dot(picked[rows, :].astype(bf16), table[:, 0:nodes], NT)
+            else:
+
+                def add(i, total):
+                    off = pl.multiple_of(i * block, block)
+                    return total + dot(picks(rows, off), table[:, pl.ds(off, block)], NT)
+
+                total = lax.fori_loop(0, blocks, add, jnp.zeros((some, table.shape[0]), f32))
             into[rows, :] = total.astype(bf16)
 
     total_counted = jnp.zeros((1, LANE), f32)
@@ -186,8 +215,33 @@
     count_high = jnp.floor(my_count * (1.0 / 256.0))
     count_low = my_count - 256.0 * count_high
 
-    table1[...] = jnp.zeros(table1.shape, bf16)
-    table1[0:fin, 0:nodes] = feat_ref[...]
+    table1[fin // 16 * 16 :, :] = jnp.zeros((fin_pad - fin // 16 * 16, nodes), bf16)
+    table1[0:fin, :] = feat_ref[...]
+
+    if picked.shape[0] == remote:
+
+        def store_picks(i, carry):
+            off = pl.multiple_of(i * 512, 512)
+            picked[:, pl.ds(off, 512)] = make_picks(row_parts[0], off, 512).astype(narrow)
+            return carry
+
+        lax.fori_loop(0, nodes // 512, store_picks, 0)
+
+    def split_in_two(value, into):
+        value = value.astype(f32)
+        largest = jnp.max(jnp.abs(value), axis=1, keepdims=True)
+        scale = jnp.ones_like(largest)
+        for power in (32, 16, 8, 4, 2, 1):
+            larger = scale * 2.0**power
+            scale = jnp.where(largest * larger <= 448.0, larger, scale)
+        scaled = value * scale
+        high = scaled.astype(narrow)
+        into[0:fin_pad, :] = high
+        into[fin_pad:, :] = ((scaled - high.astype(f32)) * 16.0).astype(narrow)
+        return 1.0 / scale
+
+    def joined_parts(both, unscale):
+        return (both[0:fin_pad, :] + both[fin_pad:, :] * (1.0 / 16.0)) * unscale
 
     wsend[...] = jnp.zeros(wsend.shape, wire)
     wsend[:, 0:fin] = first_ref[:, 0:fin].astype(bf16).astype(wire)
@@ -203,30 +257,49 @@
 
     pick_rows(table1, out1)
     spare = lax.rem(lax.broadcasted_iota(i32, (remote, fin_pad), 0), pad)
-    picked = out1[...].astype(f32)
-    picked = jnp.where(spare == pad - 2, count_high, picked)
-    picked = jnp.where(spare == pad - 1, count_low, picked)
-    out1[...] = picked.astype(bf16)
+    sent = out1[...].astype(f32)
+    sent = jnp.where(spare == pad - 2, count_high, sent)
+    sent = jnp.where(spare == pad - 1, count_low, sent)
+    out1[...] = sent.astype(bf16)
 
     pl.semaphore_wait(barrier, devices - 1)
     start_rows(out1, in1, row_ssem.at[0], row_rsem.at[0])
 
     own_chunk = pl.ds(pl.multiple_of(my_shard * chunk, chunk), chunk)
-
-    def send_weights(i, carry):
-        shard = lax.rem(my_shard + i, n_shard)
-        pltpu.make_async_remote_copy(
-            src_ref=wsend,
-            dst_ref=wwire.at[own_chunk, :],
-            send_sem=w_ssem,
-            recv_sem=w_rsem,
-            device_id=target(my_group, shard),
-            device_id_type=MESH,
-        ).start()
-        return carry
-
-    lax.fori_loop(1, n_shard, send_weights, 0)
+    weight_parts = (
+        slice(0, 4 * LANE),
+        slice(4 * LANE, 4 * LANE + 2 * hid),
+        slice(4 * LANE + 2 * hid, 4 * LANE + 4 * hid),
+    )
+
+    def send_weights(part):
+        lanes = weight_parts[part]
+
+        def start(i, carry):
+            shard = lax.rem(my_shard + i, n_shard)
+            pltpu.make_async_remote_copy(
+                src_ref=wsend.at[:, lanes],
+                dst_ref=wwire.at[own_chunk, lanes],
+                send_sem=w_ssem.at[part],
+                recv_sem=w_rsem.at[part],
+                device_id=target(my_group, shard),
+                device_id_type=MESH,
+            ).start()
+            return carry
+
+        lax.fori_loop(1, n_shard, start, 0)
+
+    def wait_weights(part):
+        lanes = weight_parts[part]
+        rows = pl.ds(0, (n_shard - 1) * chunk)
+        wait_bytes(wwire.at[rows, lanes], w_rsem.at[part])
+        wait_bytes(wwire.at[rows, lanes], w_ssem.at[part])
+        wfull[:, lanes] = wwire[:, lanes].astype(bf16)
+
     wwire[own_chunk, :] = wsend[...]
+    for part in range(3):
+        send_weights(part)
+    unscale_own = split_in_two(table1[...], first_own)
 
     high_rows = columns // LOW
     low_iota = lax.broadcasted_iota(i32, (LOW, LOW), 0).astype(f32).astype(bf16)
@@ -237,7 +310,7 @@
     zero_tile = jnp.zeros((16, LOW), bf16)
     one_low = jnp.ones((LOW, LOW), bf16)
     zero_low = jnp.zeros((LOW, LOW), bf16)
-    group_rows = 16 if counts.dtype == bf16 else 32
+    group_rows = 32
     fold = group_rows // 16
 
     def build(it, carry):
@@ -255,12 +328,12 @@
                         for h in range(high_rows)
                     ],
                     axis=0,
-                )
+                ).astype(narrow)
                 right = jnp.where(
                     low_iota == jnp.concatenate([low_row] * (LOW // 16), axis=0),
                     one_low,
                     zero_low,
-                )
+                ).astype(narrow)
                 made.append(dot(left, right, NT))
             row = pl.multiple_of(it * 128 + k * 16, group_rows)
             for h in range(high_rows):
@@ -272,14 +345,11 @@
 
     lax.fori_loop(0, nodes // 128, build, 0)
 
-    wait_bytes(wwire.at[pl.ds(0, (n_shard - 1) * chunk), :], w_rsem)
-    for _ in range(n_shard - 1):
-        wait_bytes(wsend, w_ssem)
-    wfull[...] = wwire[...].astype(bf16)
+    wait_weights(0)
     weight_lanes = (
         slice(0, 2 * LANE),
-        slice(4 * LANE, 4 * LANE + 2 * hid),
-        slice(4 * LANE + 2 * hid, 4 * LANE + 4 * hid),
+        weight_parts[1],
+        weight_parts[2],
     )
     small_full = wfull[:, 3 * LANE : 4 * LANE].astype(f32)
     for v in range(6):
@@ -292,7 +362,9 @@
     received = in1[...].astype(f32)
     scale = jnp.where(spare == pad - 2, 256.0, jnp.where(spare == pad - 1, 1.0, 0.0))
     label_count = jnp.sum(received * scale, axis=0, keepdims=True)
-    table1[:, nodes:] = in1[...].T
+    unscale_remote = split_in_two(
+        jnp.where(spare < pad - 2, received, 0.0).T, first_remote
+    )
 
     def c_block(off, lanes):
         return counts[pl.ds(off, block), lanes].astype(bf16)
@@ -302,10 +374,15 @@
     def fold_rows(value):
         return jnp.sum(value.reshape(STRIP // 8, 8, value.shape[1]), axis=0)
 
-    def activate(level, keep_slope, store_before):
+    def activate(level, keep_slope, kept, off):
         squares = jnp.zeros((8, block), f32)
         for st in strips:
-            b = before[st, :] + twice(vectors[level, st, :], block)
+            if kept is not None and keep_slope:
+                b = kept[st, pl.ds(off, block)]
+            else:
+                b = before[st, :] + twice(vectors[level, st, :], block)
+            if kept is not None and not keep_slope:
+                kept[st, pl.ds(off, block)] = b
             s = 0.5 + 0.5 * jnp.tanh(0.5 * b)
             a = b * s
             active[st, :] = a
@@ -318,19 +395,24 @@
     def hidden_strip(level, st, inverse):
         return (twice(vectors[3 + level, st, :], block) * (active[st, :] * inverse)).astype(bf16)
 
-    def forward_block(level, off, summed, table, mean, keep_slope):
+    def kept_or_none(kept):
+        return kept if kept is not None and kept.shape[1] == nodes else None
+
+    def forward_block(level, off, summed, table, mean, kept, keep_slope):
         lanes = pl.ds(off, block)
         mean_low = (summed * info[0:1, lanes]).astype(bf16)
         if mean is not None:
             mean[:, lanes] = mean_low
         joined = jnp.concatenate([table[:, lanes], mean_low], axis=0)
         before[...] = dot(matrix(level), joined, NN)
-        return joined, activate(level, keep_slope, False)
+        return joined, activate(level, keep_slope, kept_or_none(kept), off)
 
     def layer_one(i, carry):
         off = pl.multiple_of(i * block, block)
-        summed = dot(table1[...], c_block(off, slice(0, columns)), NT)
-        _, inverse = forward_block(0, off, summed, table1, mean1, False)
+        own = dot(first_own[...], counts[pl.ds(off, block), 0:nodes], NT)
+        away = dot(first_remote[...], counts[pl.ds(off, block), nodes:], NT)
+        summed = joined_parts(own, unscale_own) + joined_parts(away, unscale_remote)
+        _, inverse = forward_block(0, off, summed, table1, mean1, before1, False)
         for st in strips:
             table2[st, pl.ds(off, block)] = hidden_strip(0, st, inverse)
         return carry
@@ -349,10 +431,10 @@
 
     def exchange_forward(table, x):
         pick_rows(table, outs)
-        start_rows(outs, ins.at[x], row_ssem.at[x + 1], row_rsem.at[x + 1])
+        start_rows(outs, ins.at[x % 2], row_ssem.at[x + 1], row_rsem.at[x + 1])
         own_sums(table)
-        wait_rows(outs, ins.at[x], row_ssem.at[x + 1], row_rsem.at[x + 1])
-        table[:, nodes:] = ins[x].T
+        wait_rows(outs, ins.at[x % 2], row_ssem.at[x + 1], row_rsem.at[x + 1])
+        table[:, nodes:] = ins[x % 2].T
 
     def all_sums(table, off):
         return wide[:, pl.ds(off, block)] + dot(
@@ -360,10 +442,11 @@
         )
 
     exchange_forward(table2, 0)
+    wait_weights(1)
 
     def layer_two(i, carry):
         off = pl.multiple_of(i * block, block)
-        _, inverse = forward_block(1, off, all_sums(table2, off), table2, mean2, False)
+        _, inverse = forward_block(1, off, all_sums(table2, off), table2, mean2, before2, False)
         for st in strips:
             table3[st, pl.ds(off, block)] = hidden_strip(1, st, inverse)
         return carry
@@ -371,6 +454,9 @@
     lax.fori_loop(0, blocks, layer_two, 0)
 
     exchange_forward(table3, 1)
+    wait_weights(2)
+    gfirst[...] = jnp.zeros(gfirst.shape, f32)
+    ghead[...] = jnp.zeros(ghead.shape, f32)
     gfull[...] = jnp.zeros(gfull.shape, f32)
     gacc[...] = jnp.zeros(gacc.shape, f32)
     bacc[...] = jnp.zeros(bacc.shape, f32)
@@ -404,11 +490,10 @@
             gacc[level, st, :] += gain_sum
             bacc[level, st, :] += bias_sum
         low = jnp.concatenate(low_parts, axis=0)
-        seg = (0, 1, 2)[level]
-        pieces = joined.shape[0] // LANE
+        into = gfirst if level == 0 else gfull.at[level - 1]
         added = dot(low, joined, NT)
-        for j in range(pieces):
-            gfull[seg, j] += added[:, j * LANE : (j + 1) * LANE]
+        for j in range(joined.shape[0] // LANE):
+            into[j] += added[:, j * LANE : (j + 1) * LANE]
         if need_input:
             back = dot(matrix(level), low, TN)
             wide[:, lanes] = back[0:hid, :]
@@ -417,7 +502,7 @@
     def layer_three(i, loss):
         off = pl.multiple_of(i * block, block)
         lanes = pl.ds(off, block)
-        joined, inverse = forward_block(2, off, all_sums(table3, off), table3, None, True)
+        joined, inverse = forward_block(2, off, all_sums(table3, off), table3, None, None, True)
         last = jnp.concatenate([hidden_strip(2, st, inverse) for st in strips], axis=0)
         logits = dot(head_low, last, TN)[0:cls_pad, :]
         logits = jnp.where(class_iota < cls, logits, -jnp.inf)
@@ -433,7 +518,7 @@
         g_low = jnp.concatenate(
             [g_logits, jnp.zeros((LANE - cls_pad, block), f32)], axis=0
         ).astype(bf16)
-        gfull[0, 2] += dot(last, g_low, NT)
+        ghead[...] += dot(last, g_low, NT)
         ghid[...] = dot(head_low, g_low, NN)
         backward_block(2, off, joined, inverse, True)
         return loss
@@ -512,12 +597,131 @@
             wait_bytes(part3.at[seg], g_ssem.at[2, seg])
         wait_bytes(recv3.at[seg, pl.ds(0, n_group - 1)], g_rsem.at[2, seg])
 
-    def exchange_backward(x):
+    def bias_and_gain(levels, first_lane):
+        lane_wide = lax.broadcasted_iota(i32, (hid, LANE), 1)
+        total = jnp.zeros((hid, LANE), f32)
+        for n, level in enumerate(levels):
+            for acc, shift in ((bacc, 0), (gacc, len(levels))):
+                total = jnp.where(
+                    lane_wide == first_lane + shift + n,
+                    jnp.sum(acc[level], axis=1, keepdims=True),
+                    total,
+                )
+        return total
+
+    def start_head():
+        total = ghead[...] + bias_and_gain((1, 2), cls)
+        ghead[...] = total
+        hwire[...] = total.astype(wire).reshape(n_shard, chunk, LANE)
+
+        def start(i, carry):
+            shard = lax.rem(my_shard + i, n_shard)
+            pltpu.make_async_remote_copy(
+                src_ref=hwire.at[shard],
+                dst_ref=hrecv.at[my_shard],
+                send_sem=h_ssem.at[0],
+                recv_sem=h_rsem.at[0],
+                device_id=target(my_group, shard),
+                device_id_type=MESH,
+            ).start()
+            return carry
+
+        lax.fori_loop(1, n_shard, start, 0)
+        hrecv[my_shard] = jnp.zeros(hrecv.shape[1:], wire)
+
+    def share_head():
+        wait_bytes(hwire.at[pl.ds(0, n_shard - 1)], h_ssem.at[0])
+        wait_bytes(hrecv.at[pl.ds(0, n_shard - 1)], h_rsem.at[0])
+        total = ghead[own_chunk, :]
+        for shard in range(n_shard):
+            total = total + hrecv[shard].astype(f32)
+        hpart[...] = total
+
+        def start(i, carry):
+            group = lax.rem(my_group + i, n_group)
+            pltpu.make_async_remote_copy(
+                src_ref=hpart,
+                dst_ref=hfinal.at[my_group],
+                send_sem=h_ssem.at[1],
+                recv_sem=h_rsem.at[1],
+                device_id=target(group, my_shard),
+                device_id_type=MESH,
+            ).start()
+            return carry
+
+        lax.fori_loop(1, n_group, start, 0)
+        hfinal[my_group] = total
+
+    def wait_head():
+        wait_bytes(hfinal.at[pl.ds(0, n_group - 1)], h_ssem.at[1])
+        wait_bytes(hfinal.at[pl.ds(0, n_group - 1)], h_rsem.at[1])
+        total = hfinal[0]
+        for group in range(1, n_group):
+            total = total + hfinal[group]
+        head_out[...] = total
+        return jnp.sum(total * total) * (1.0 / n_group)
+
+    units, unit_rows, row_parts_first = cfg["units"], cfg["unit_rows"], cfg["units"] // 2
+
+    def start_first_layer():
+        gfirst[0] += bias_and_gain((0,), fin)
+        for unit in range(units):
+            tile, part = unit // row_parts_first, unit % row_parts_first
+            whole = gfirst[tile].reshape(n_shard, chunk, LANE)
+            fwire[unit] = whole[:, part * unit_rows : (part + 1) * unit_rows, :].astype(wire)
+
+        def start(i, carry):
+            peer = lax.rem(me + i, devices)
+            group, shard = lax.div(peer, n_shard), lax.rem(peer, n_shard)
+            pltpu.make_async_remote_copy(
+                src_ref=fwire.at[lax.rem(group, units), shard],
+                dst_ref=frecv.at[me],
+                send_sem=f_ssem.at[0],
+                recv_sem=f_rsem.at[0],
+                device_id=target(group, shard),
+                device_id_type=MESH,
+            ).start()
+            return carry
+
+        lax.fori_loop(1, devices, start, 0)
+        frecv[me] = fwire[lax.rem(my_group, units), my_shard]
+
+    def share_first_layer():
+        wait_bytes(frecv.at[pl.ds(0, devices - 1)], f_ssem.at[0])
+        wait_bytes(frecv.at[pl.ds(0, devices - 1)], f_rsem.at[0])
+        total = jnp.sum(frecv[...].astype(f32), axis=0)
+        fpart[...] = total
+
+        def start(i, carry):
+            group = lax.rem(my_group + i, n_group)
+            pltpu.make_async_remote_copy(
+                src_ref=fpart,
+                dst_ref=ffinal.at[my_group],
+                send_sem=f_ssem.at[1],
+                recv_sem=f_rsem.at[1],
+                device_id=target(group, my_shard),
+                device_id_type=MESH,
+            ).start()
+            return carry
+
+        lax.fori_loop(1, n_group, start, 0)
+        ffinal[my_group] = total
+        return jnp.sum(total * total) * (units / n_group)
+
+    def wait_first_layer():
+        wait_bytes(ffinal.at[pl.ds(0, n_group - 1)], f_ssem.at[1])
+        wait_bytes(ffinal.at[pl.ds(0, n_group - 1)], f_rsem.at[1])
+        for unit in range(units):
+            tile, part = unit // row_parts_first, unit % row_parts_first
+            first_out[tile, part * unit_rows : (part + 1) * unit_rows, :] = ffinal[unit]
+
+    def exchange_backward(x, meanwhile):
         for rows in row_parts:
             lanes = slice(nodes + rows.start, nodes + rows.stop)
             back = dot(gmean[...], counts[:, lanes].astype(bf16), NN)
             outs[rows, :] = back.astype(bf16).T
-        start_rows(outs, ins.at[x], row_ssem.at[x + 1], row_rsem.at[x + 1])
+        start_rows(outs, ins.at[x % 2], row_ssem.at[x + 1], row_rsem.at[x + 1])
+        meanwhile()
 
         def add(i, carry):
             off = pl.multiple_of(i * block, block)
@@ -526,70 +730,64 @@
             return carry
 
         lax.fori_loop(0, blocks, add, 0)
-        wait_rows(outs, ins.at[x], row_ssem.at[x + 1], row_rsem.at[x + 1])
-
-    def returned(x, i):
-        off = pl.multiple_of(i * block, block)
+        wait_rows(outs, ins.at[x % 2], row_ssem.at[x + 1], row_rsem.at[x + 1])
+
+    def returned(x, off):
         total = wide[:, pl.ds(off, block)]
         for rows in row_parts:
-            total = total + dot(ins[x, rows, :], picks(i, rows), TN)
+            total = total + dot(ins[x % 2, rows, :], picks(rows, off), TN)
         return total
 
-    start_first(2)
-    exchange_backward(2)
-    start_second(2)
+    exchange_backward(2, lambda: start_first(1))
+    start_second(1)
 
     def backward_two(i, carry):
         off = pl.multiple_of(i * block, block)
         lanes = pl.ds(off, block)
-        ghid[...] = returned(2, i)
+        ghid[...] = returned(2, off)
         joined = jnp.concatenate([table2[:, lanes], mean2[:, lanes]], axis=0)
-        before[...] = dot(matrix(1), joined, NN)
-        inverse = activate(1, True, False)
+        if before2.shape[1] < nodes:
+            before[...] = dot(matrix(1), joined, NN)
+        inverse = activate(1, True, kept_or_none(before2), off)
         backward_block(1, off, joined, inverse, True)
         return carry
 
     lax.fori_loop(0, blocks, backward_two, 0)
-    start_first(1)
-    square = start_third(2)
-    exchange_backward(3)
-    start_second(1)
+
+    def meanwhile():
+        start_first(0)
+        start_head()
+
+    exchange_backward(3, meanwhile)
+    square = start_third(1)
+    start_second(0)
+    share_head()
 
     def backward_one(i, carry):
         off = pl.multiple_of(i * block, block)
         lanes = pl.ds(off, block)
-        ghid[...] = returned(3, i)
+        ghid[...] = returned(3, off)
         joined = jnp.concatenate([table1[:, lanes], mean1[:, lanes]], axis=0)
-        before[...] = dot(matrix(0), joined, NN)
-        inverse = activate(0, True, False)
+        if before1.shape[1] < nodes:
+            before[...] = dot(matrix(0), joined, NN)
+        inverse = activate(0, True, kept_or_none(before1), off)
         backward_block(0, off, joined, inverse, False)
         return carry
 
     lax.fori_loop(0, blocks, backward_one, 0)
-    lane_wide = lax.broadcasted_iota(i32, (hid, LANE), 1)
-    small_grad = jnp.zeros((hid, LANE), f32)
-    for level in range(3):
-        small_grad = jnp.where(
-            lane_wide == level, jnp.sum(bacc[level], axis=1, keepdims=True), small_grad
-        )
-        small_grad = jnp.where(
-            lane_wide == 3 + level, jnp.sum(gacc[level], axis=1, keepdims=True), small_grad
-        )
-    gfull[0, 3] = small_grad
-    start_first(0)
-    square = square + start_third(1)
-    start_second(0)
-    square = square + start_third(0)
-
-    row8 = lax.broadcasted_iota(i32, (8, LANE), 0)
-    mine = jnp.where(row8 == 0, square, jnp.where(row8 == 1, jnp.sum(loss), 0.0))
+    start_first_layer()
+    square = square + start_third(0) + wait_head()
+    square = square + share_first_layer()
+
+    lane_of = lax.broadcasted_iota(i32, (8, LANE), 1)
+    mine = jnp.where(lane_of == 0, square, jnp.where(lane_of == 1, jnp.sum(loss), 0.0))
     scal_send[...] = mine
 
     def send_scalars(i, carry):
         peer = lax.rem(me + i, devices)
         pltpu.make_async_remote_copy(
-            src_ref=scal_send,
-            dst_ref=scal_recv.at[me],
+            src_ref=scal_send.at[pl.ds(0, 1), :],
+            dst_ref=scal_recv.at[pl.ds(me, 1), :],
             send_sem=s_ssem,
             recv_sem=s_rsem,
             device_id=target(lax.div(peer, n_shard), lax.rem(peer, n_shard)),
@@ -598,20 +796,15 @@
         return carry
 
     lax.fori_loop(1, devices, send_scalars, 0)
-    scal_recv[me] = mine
-    for seg in range(3):
+    scal_recv[pl.ds(me, 1), :] = mine[0:1, :]
+    for seg in range(2):
         wait_third(seg)
-    grad_out[...] = recv3[...]
-    wait_bytes(scal_recv.at[pl.ds(0, devices - 1)], s_rsem)
-
-    def drain(i, carry):
-        wait_bytes(scal_send, s_ssem)
-        return carry
-
-    lax.fori_loop(1, devices, drain, 0)
-    scalar_out[...] = jnp.where(
-        row8 == 2, label_count[0:1, 0:1], jnp.sum(scal_recv[...], axis=0)
-    )
+    part_out[...] = recv3[...]
+    wait_first_layer()
+    wait_bytes(scal_recv.at[pl.ds(0, devices - 1), :], s_rsem)
+    wait_bytes(scal_recv.at[pl.ds(0, devices - 1), :], s_ssem)
+    totals = jnp.sum(scal_recv[...], axis=0, keepdims=True)
+    scalar_out[...] = jnp.where(lane_of == 2, label_count[0:1, 0:1], totals)
 
 
 def adamw(weight, grad, moment, square, rate, decay):
@@ -623,6 +816,45 @@
         moment_hat / (jnp.sqrt(square_hat) + adam_epsilon) + decay * weight
     )
     return (weight_new, moment_new, square_new)
+
+
+def update_kernel(fin, cls, part_ref, head_ref, first_ref, scalar_ref, *refs):
+    states = [refs[3 * k : 3 * k + 3] for k in range(5)]
+    outs = [refs[15 + 3 * k : 18 + 3 * k] for k in range(5)]
+    copies = refs[30:33]
+    loss_out, count_out, norm_out = refs[33:36]
+    norm = jnp.sqrt(scalar_ref[0:1, 0:1])
+    loss_out[...] = scalar_ref[0:1, 1:2]
+    count_out[...] = scalar_ref[0:1, 2:3]
+    norm_out[...] = norm
+    factor = jnp.minimum(1.0, threshold / norm)
+    small_last = head_ref[...].T
+    small_first = first_ref[0].T
+    bias = jnp.concatenate([small_first[fin : fin + 1], small_last[cls : cls + 2]], axis=0)
+    gain = jnp.concatenate(
+        [small_first[fin + 1 : fin + 2], small_last[cls + 2 : cls + 4]], axis=0
+    )
+
+    def update(k, grad, where, rate, decay):
+        news = adamw(
+            states[k][0][where], grad * factor, states[k][1][where], states[k][2][where], rate, decay
+        )
+        for out, new in zip(outs[k], news):
+            out[where] = new
+        if k < 3:
+            copies[k][where] = news[0].astype(bf16)
+
+    everything = (slice(None), slice(None))
+    update(0, first_ref[0][:, 0:fin], (slice(None), slice(0, fin)), 0.05, 0.01)
+    update(0, first_ref[1][:, 0:fin], (slice(None), slice(fin, 2 * fin)), 0.05, 0.01)
+    n_group = part_ref.shape[1]
+    for level in range(2):
+        for piece in range(n_group):
+            lanes = slice(piece * LANE, (piece + 1) * LANE)
+            update(1, part_ref[level, piece], (level, slice(None), lanes), 0.05, 0.01)
+    update(2, head_ref[:, 0:cls], everything, 0.05, 0.01)
+    update(3, bias, everything, 0.3, 0.0)
+    update(4, gain, everything, 0.3, 0.0)
 
 
 def per_device(
@@ -661,9 +893,11 @@
     pad = round_up(cap + 2, 16)
     remote = devices * pad
     columns = nodes + remote
-    block = 256
+    block = 1024 if remote <= 512 else 512
     wire = bf16 if chunk % 16 == 0 else f32
-    counts_dtype = bf16 if nodes * columns * 2 <= 40 * 2**20 else jnp.float8_e4m3fn
+    least = 16 if wire == bf16 else 8
+    units = n_group if chunk * 2 // n_group >= least else 2
+    unit_rows = chunk * 2 // units
     fin_pad = LANE
     cfg = dict(
         n_group=n_group,
@@ -678,6 +912,8 @@
         block=block,
         fin_pad=fin_pad,
         hid=hid,
+        units=units,
+        unit_rows=unit_rows,
     )
 
     away = neighbours - nodes
@@ -693,19 +929,26 @@
     smem = pl.BlockSpec(memory_space=pltpu.SMEM)
     width = 4 * LANE + 4 * hid
     dma = pltpu.SemaphoreType.DMA
+    stored = remote if remote <= 512 else 32
+    kept_nodes = nodes if remote <= 512 else LANE
     scratch = [
-        pltpu.VMEM((nodes, columns), counts_dtype),
-        pltpu.VMEM((fin_pad, columns), bf16),
+        pltpu.VMEM((nodes, columns), narrow),
+        pltpu.VMEM((stored, nodes), narrow),
+        pltpu.VMEM((fin_pad, nodes), bf16),
         pltpu.VMEM((hid, columns), bf16),
         pltpu.VMEM((hid, columns), bf16),
+        pltpu.VMEM((2 * fin_pad, nodes), narrow),
+        pltpu.VMEM((2 * fin_pad, remote), narrow),
         pltpu.VMEM((fin_pad, nodes), bf16),
         pltpu.VMEM((hid, nodes), bf16),
+        pltpu.VMEM((hid, kept_nodes), f32),
+        pltpu.VMEM((hid, kept_nodes), f32),
         pltpu.VMEM((hid, nodes), bf16),
         pltpu.VMEM((hid, nodes), f32),
         pltpu.VMEM((remote, fin_pad), bf16),
         pltpu.VMEM((remote, fin_pad), bf16),
         pltpu.VMEM((remote, hid), bf16),
-        pltpu.VMEM((4, remote, hid), bf16),
+        pltpu.VMEM((2, remote, hid), bf16),
         pltpu.VMEM((8, nodes), f32),
         pltpu.VMEM((chunk, width), wire),
         pltpu.VMEM((hid, width), wire),
@@ -717,33 +960,48 @@
         pltpu.VMEM((hid, block), f32),
         pltpu.VMEM((3, hid, LANE), f32),
         pltpu.VMEM((3, hid, LANE), f32),
+        pltpu.VMEM((2, n_group, hid, LANE), f32),
+        pltpu.VMEM((2, n_group, hid, LANE), wire),
+        pltpu.VMEM((2, n_group, hid, LANE), wire),
+        pltpu.VMEM((2, n_shard, chunk, LANE), wire),
+        pltpu.VMEM((2, n_shard, chunk, LANE), wire),
+        pltpu.VMEM((2, chunk, LANE), f32),
+        pltpu.VMEM((2, n_group, chunk, LANE), f32),
+        pltpu.VMEM((2, hid, LANE), f32),
+        pltpu.VMEM((units, n_shard, unit_rows, LANE), wire),
+        pltpu.VMEM((devices, unit_rows, LANE), wire),
+        pltpu.VMEM((unit_rows, LANE), f32),
+        pltpu.VMEM((n_group, unit_rows, LANE), f32),
+        pltpu.VMEM((hid, LANE), f32),
+        pltpu.VMEM((n_shard, chunk, LANE), wire),
+        pltpu.VMEM((n_shard, chunk, LANE), wire),
+        pltpu.VMEM((chunk, LANE), f32),
+        pltpu.VMEM((n_group, chunk, LANE), f32),
         pltpu.VMEM((8, LANE), f32),
-        pltpu.VMEM((3, n_group, hid, LANE), f32),
-        pltpu.VMEM((3, n_group, hid, LANE), wire),
-        pltpu.VMEM((3, n_group, hid, LANE), wire),
-        pltpu.VMEM((3, n_shard, chunk, LANE), wire),
-        pltpu.VMEM((3, n_shard, chunk, LANE), wire),
-        pltpu.VMEM((3, chunk, LANE), f32),
-        pltpu.VMEM((3, n_group, chunk, LANE), f32),
-        pltpu.VMEM((8, LANE), f32),
-        pltpu.VMEM((devices, 8, LANE), f32),
+        pltpu.VMEM((devices, LANE), f32),
         dma((5,)),
         dma((5,)),
-        dma,
-        dma,
-        dma((3, 3)),
-        dma((3, 3)),
+        dma((3,)),
+        dma((3,)),
+        dma((3, 2)),
+        dma((3, 2)),
+        dma((2,)),
+        dma((2,)),
+        dma((2,)),
+        dma((2,)),
         dma,
         dma,
     ]
-    grads, scalars = pl.pallas_call(
+    sums = pl.pallas_call(
         functools.partial(step_kernel, cfg),
         out_shape=(
-            jax.ShapeDtypeStruct((3, n_group, chunk, LANE), f32),
+            jax.ShapeDtypeStruct((2, n_group, chunk, LANE), f32),
+            jax.ShapeDtypeStruct((chunk, LANE), f32),
+            jax.ShapeDtypeStruct((2, chunk, LANE), f32),
             jax.ShapeDtypeStruct((8, LANE), f32),
         ),
         in_specs=[vmem] * 5 + [smem] + [vmem] * 6,
-        out_specs=(vmem, vmem),
+        out_specs=(vmem,) * 4,
         scratch_shapes=scratch,
         compiler_params=pltpu.CompilerParams(
             collective_id=0, has_side_effects=True, vmem_limit_bytes=63 * 2**20
@@ -762,32 +1020,30 @@
         biases,
         gains,
     )
-    grad_norm = jnp.sqrt(scalars[0, 0])
-    loss_sum = scalars[1, 0]
-    label_count = scalars[2, 0]
-    factor = jnp.minimum(1.0, threshold / grad_norm)
-    grads = grads * factor
-    grad_first = jnp.concatenate([grads[0, 0, :, :fin], grads[0, 1, :, :fin]], axis=1).T
-    grad_rest = jnp.stack(
-        [jnp.concatenate([grads[s, j] for j in range(n_group)], axis=1).T for s in (1, 2)]
+    turned = lambda value: value.T
+    turned_rest = lambda value: value.transpose(0, 2, 1)
+    same = lambda value: value
+    turns = (turned, turned_rest, same, same, same)
+    states = (
+        (weight_first, moment_first, square_first),
+        (weight_rest, moment_rest, square_rest),
+        (weight_head, moment_head, square_head),
+        (biases, moment_bias, square_bias),
+        (gains, moment_gain, square_gain),
     )
-    grad_head = grads[0, 2, :, :cls]
-    grad_bias = grads[0, 3, :, 0:3].T
-    grad_gain = grads[0, 3, :, 3:6].T
-    first_out = adamw(weight_first, grad_first, moment_first, square_first, 0.05, 0.01)
-    rest_out = adamw(weight_rest, grad_rest, moment_rest, square_rest, 0.05, 0.01)
-    head_out = adamw(weight_head, grad_head, moment_head, square_head, 0.05, 0.01)
-    bias_out = adamw(biases, grad_bias, moment_bias, square_bias, 0.3, 0.0)
-    gain_out = adamw(gains, grad_gain, moment_gain, square_gain, 0.3, 0.0)
-    return (
-        (loss_sum, label_count, grad_norm)
-        + first_out
-        + rest_out
-        + head_out
-        + bias_out
-        + gain_out
-        + (first_out[0].astype(bf16), rest_out[0].astype(bf16), head_out[0].astype(bf16))
-    )
+    flat = [turn(value) for turn, three in zip(turns, states) for value in three]
+    shapes = [jax.ShapeDtypeStruct(value.shape, f32) for value in flat]
+    shapes += [jax.ShapeDtypeStruct(flat[3 * k].shape, bf16) for k in range(3)]
+    shapes += [jax.ShapeDtypeStruct((1, 1), f32)] * 3
+    updated = pl.pallas_call(
+        functools.partial(update_kernel, fin, cls),
+        out_shape=tuple(shapes),
+        in_specs=[vmem] * (4 + len(flat)),
+        out_specs=(vmem,) * len(shapes),
+    )(*sums, *flat)
+    news = tuple(turns[k // 3](updated[k]) for k in range(15))
+    copies = tuple(turns[k](updated[15 + k]) for k in range(3))
+    return tuple(value.reshape(()) for value in updated[18:]) + news + copies
 
 
 def solution(mesh):

time: 193 us -> 121 us (0.63)
  Pallas kernels: 180 us -> 115 us
  other arithmetic: 4.95 us -> 1.2 us
    pallas_call x1, Pallas kernels: 180 us -> 113 us  [per_device(): pl.pallas_call(functools.partial(step_kernel, cfg), out_shape=(jax.ShapeD...]
    pallas_call x0 -> x1, Pallas kernels: none -> 2.35 us  [per_device(): pl.pallas_call(functools.partial(update_kernel, fin, cls), out_shape=tupl...]
    convert_element_type x3 -> x0, other arithmetic: 2.18 us -> none  [the longest x1 0.82 us: per_device(): rest_out[0].astype(bf16)]
where the time goes in v2:
time: 121 us
  Pallas kernels  115 us (95%)
  local copies, waits for them, and re-layouts  3.15 us (3%)
  between operations  1.5 us (1%)
    pallas_call x1, Pallas kernels, per_device(): pl.pallas_call(functools.partial(step_kernel, cfg), out_shape=(jax.ShapeD...  113 us

profile of v2, /device:TPU:0, one launch (start us, length us, event | category | flops | bytes accessed | tf_op | source)
XLA Modules:
  0.0 121.3 jit_solution(7397139352101231717)
XLA Ops:
  0.7 1.2 select_select_fusion
  1.9 0.0 copy-start
  1.9 0.6 copy.44
  2.5 1.5 %reshape.66.key_ref = s32[256,256]{1,0:T(8,128)} reshape(s32[4096,16]{1,0:T(8,128)S(1)} %copy.44) | data formatting | bytes 524288 | tf_op jit(solution)/shard_map/reshape | solution.py:924
  4.0 0.0 copy-done
  4.0 0.1 copy.46
  4.1 0.1 broadcast_in_dim.10
  4.2 0.8 broadcast_in_dim.11.send_ref
  5.7 113.1 %shard_map.373 = (f32[2,4,32,128]{3,2,1,0:T(8,128)}, f32[32,128]{1,0:T(8,128)}, f32[2,32,128]{2,1,0:T(8,128)}, f32[8,128]{1,0:T(8,128)}) custom-call(bf16[100,4096]{1,0:T(8,128)(2,1)} %bitcast.21, s32[256,256]{1,0:T(8,128)} %reshape.66.key_ref, s32[32,128]{1,0:T(8,128)} %bitcast.28, s32[32,128]{1,0:T(8,128)} %bitcast.31, s32[32,128]{1,0:T(8,128)} %bitcast.32, ...), custom_call_target="tpu_custom_call" | custom-call | tf_op jit(solution)/shard_map/pallas_call | solution.py:995
  118.8 2.3 %shard_map.374 = (f32[32,200]{1,0:T(8,128)}, f32[32,200]{1,0:T(8,128)}, f32[32,200]{1,0:T(8,128)}, f32[2,32,512]{2,1,0:T(8,128)}, f32[2,32,512]{2,1,0:T(8,128)},...) custom-call(f32[2,4,32,128]{3,2,1,0:T(8,128)} %get-tuple-element.46., ...), custom_call_target="tpu_custom_call" | custom-call | tf_op jit(solution)/shard_map/pallas_call | solution.py:1038
  (1 shorter events, 0.0 us)
Async XLA Ops:
  1.9 2.1 %copy-start = (s32[32,12]{0,1:T(8,128)S(1)}, s32[32,12]{0,1:T(8,128)}, u32[]{:S(2)}) copy-start(s32[32,12]{0,1:T(8,128)} %param.26) | copy-start | bytes 4612

commit v3 on v2

--- a/solution.py
+++ b/solution.py
@@ -44,7 +44,7 @@
 def step_kernel(
     cfg,
     feat_ref,
-    key_ref,
+    neighbour_ref,
     deg_ref,
     label_ref,
     mask_ref,
@@ -61,6 +61,10 @@
     scalar_out,
     counts,
     picked,
+    send_columns,
+    slot_rows,
+    key_high,
+    key_low,
     table1,
     table2,
     table3,
@@ -72,8 +76,6 @@
     before2,
     gmean,
     wide,
-    out1,
-    in1,
     outs,
     ins,
     info,
@@ -132,6 +134,8 @@
     def target(group, shard):
         return {"group": group, "shard": shard}
 
+    out1, in1 = outs.at[:, pl.ds(0, fin_pad)], ins.at[1, :, pl.ds(0, fin_pad)]
+
     barrier = pltpu.get_barrier_semaphore()
 
     def greet(i, carry):
@@ -177,7 +181,7 @@
     def make_picks(rows, off, width):
         lanes = lax.broadcasted_iota(i32, (some, LANE), 1) + off
         parts = [
-            jnp.where(send_ref[rows, :] == lanes + LANE * j, 1.0, 0.0).astype(bf16)
+            jnp.where(send_columns[rows, :] == lanes + LANE * j, 1.0, 0.0).astype(bf16)
             for j in range(width // LANE)
         ]
         return jnp.concatenate(parts, axis=1)
@@ -204,7 +208,9 @@
     lane_row = lax.broadcasted_iota(i32, (1, LANE), 1)
     for r in range(nodes // LANE):
         lanes = slice(r * LANE, (r + 1) * LANE)
-        info[0:1, lanes] = 1.0 / deg_ref[r : r + 1, :].astype(f32)
+        degree = deg_ref[r : r + 1, :].astype(f32)
+        info[0:1, lanes] = 1.0 / degree
+        info[3:4, lanes] = degree
         info[1:2, lanes] = label_ref[r : r + 1, :].astype(f32)
         counted = jnp.where(
             (lane_row + r * LANE < count_ref[0]) & (mask_ref[r : r + 1, :] > 0), 1.0, 0.0
@@ -217,15 +223,6 @@
 
     table1[fin // 16 * 16 :, :] = jnp.zeros((fin_pad - fin // 16 * 16, nodes), bf16)
     table1[0:fin, :] = feat_ref[...]
-
-    if picked.shape[0] == remote:
-
-        def store_picks(i, carry):
-            off = pl.multiple_of(i * 512, 512)
-            picked[:, pl.ds(off, 512)] = make_picks(row_parts[0], off, 512).astype(narrow)
-            return carry
-
-        lax.fori_loop(0, nodes // 512, store_picks, 0)
 
     def split_in_two(value, into):
         value = value.astype(f32)
@@ -243,17 +240,43 @@
     def joined_parts(both, unscale):
         return (both[0:fin_pad, :] + both[fin_pad:, :] * (1.0 / 16.0)) * unscale
 
+    cap, slots = cfg["cap"], cfg["slots"]
+    numbers = jnp.concatenate(
+        [send_ref[...], jnp.full((pad - cap, devices), -256, i32)], axis=0
+    )
+    halves = jnp.concatenate([numbers >> 8, numbers & 255], axis=0).astype(f32).astype(bf16)
+    for rows in row_parts:
+        peers = lax.broadcasted_iota(i32, (some, devices), 1)
+        row_numbers = lax.broadcasted_iota(i32, (some, devices), 0) + rows.start
+        chosen = jnp.where(lax.div(row_numbers, pad) == peers, 1.0, 0.0).astype(bf16)
+        found = dot(chosen, halves, NT)
+        lanes = lax.broadcasted_iota(i32, (some, 2 * pad), 1)
+        place = lax.rem(lax.broadcasted_iota(i32, (some, 2 * pad), 0), pad)
+        found = jnp.where(lanes < pad, 256.0 * found, found)
+        found = jnp.where(lax.rem(lanes, pad) == place, found, 0.0)
+        column = jnp.sum(found, axis=1, keepdims=True).astype(i32)
+        send_columns[rows, :] = jnp.broadcast_to(column, (some, LANE))
+
     wsend[...] = jnp.zeros(wsend.shape, wire)
     wsend[:, 0:fin] = first_ref[:, 0:fin].astype(bf16).astype(wire)
     wsend[:, LANE : LANE + fin] = first_ref[:, fin : 2 * fin].astype(bf16).astype(wire)
-    wsend[:, 2 * LANE : 2 * LANE + cls] = head_ref[...].astype(bf16).astype(wire)
+    wsend[:, 3 * LANE + 4 * hid : 3 * LANE + 4 * hid + cls] = head_ref[...].astype(bf16).astype(wire)
     small = jnp.concatenate(
         [bias_ref[...], gain_ref[...], jnp.zeros((2, chunk), f32)], axis=0
     )
-    wsend[:, 3 * LANE : 3 * LANE + 8] = small.T.astype(bf16).astype(wire)
+    wsend[:, 2 * LANE : 2 * LANE + 8] = small.T.astype(bf16).astype(wire)
     for level in range(2):
-        lanes = slice(4 * LANE + level * 2 * hid, 4 * LANE + (level + 1) * 2 * hid)
+        lanes = slice(3 * LANE + level * 2 * hid, 3 * LANE + (level + 1) * 2 * hid)
         wsend[:, lanes] = rest_ref[level].astype(bf16).astype(wire)
+
+    if picked.shape[0] == remote:
+
+        def store_picks(i, carry):
+            off = pl.multiple_of(i * 512, 512)
+            picked[:, pl.ds(off, 512)] = make_picks(row_parts[0], off, 512).astype(narrow)
+            return carry
+
+        lax.fori_loop(0, nodes // 512, store_picks, 0)
 
     pick_rows(table1, out1)
     spare = lax.rem(lax.broadcasted_iota(i32, (remote, fin_pad), 0), pad)
@@ -262,14 +285,11 @@
     sent = jnp.where(spare == pad - 1, count_low, sent)
     out1[...] = sent.astype(bf16)
 
-    pl.semaphore_wait(barrier, devices - 1)
-    start_rows(out1, in1, row_ssem.at[0], row_rsem.at[0])
-
     own_chunk = pl.ds(pl.multiple_of(my_shard * chunk, chunk), chunk)
     weight_parts = (
-        slice(0, 4 * LANE),
-        slice(4 * LANE, 4 * LANE + 2 * hid),
-        slice(4 * LANE + 2 * hid, 4 * LANE + 4 * hid),
+        slice(0, 3 * LANE),
+        slice(3 * LANE, 3 * LANE + 2 * hid),
+        slice(3 * LANE + 2 * hid, 4 * LANE + 4 * hid),
     )
 
     def send_weights(part):
@@ -296,15 +316,39 @@
         wait_bytes(wwire.at[rows, lanes], w_ssem.at[part])
         wfull[:, lanes] = wwire[:, lanes].astype(bf16)
 
+    pl.semaphore_wait(barrier, devices - 1)
+    start_rows(out1, in1, row_ssem.at[0], row_rsem.at[0])
     wwire[own_chunk, :] = wsend[...]
-    for part in range(3):
-        send_weights(part)
-    unscale_own = split_in_two(table1[...], first_own)
+    send_weights(0)
+
+    tiles = nodes // LANE
+    for g in range(tiles):
+        lanes = slice(g * LANE, (g + 1) * LANE)
+        column = neighbour_ref[:, lanes]
+        away = column - nodes
+        source = ((away.astype(f32) + 0.5) * (1.0 / cap)).astype(i32)
+        moved = jnp.where(away < 0, column, column + source * (pad - cap))
+        live = lax.broadcasted_iota(i32, (slots, LANE), 0).astype(f32) < info[3:4, lanes]
+        slot_rows[g * slots : (g + 1) * slots, :] = jnp.where(live, moved, -256)
+    per_half = LANE // 16
+    sixteenth = lax.div(lax.broadcasted_iota(i32, (tiles, LANE), 1), 16)
+    for half in range(slots // per_half):
+        made = [jnp.zeros((tiles, LANE), i32)] * per_half
+        for j in range(per_half):
+            rows = slot_rows[pl.ds(half * per_half + j, tiles, stride=slots), :]
+            here = sixteenth == j
+            for b in range(per_half):
+                turned = pltpu.roll(rows, 16 * ((j - b) % per_half), 1) if j != b else rows
+                made[b] = jnp.where(here, turned, made[b])
+        lanes = slice(half * LANE, (half + 1) * LANE)
+        for b in range(per_half):
+            key_high[b, :, lanes] = (made[b] >> 8).astype(f32)
+            key_low[b, :, lanes] = (made[b] & 255).astype(f32)
 
     high_rows = columns // LOW
     low_iota = lax.broadcasted_iota(i32, (LOW, LOW), 0).astype(f32).astype(bf16)
     same_node = (
-        lax.div(lax.broadcasted_iota(i32, (16, LOW), 1), 16)
+        lax.rem(lax.broadcasted_iota(i32, (16, LOW), 1), 16)
         == lax.broadcasted_iota(i32, (16, LOW), 0)
     ).astype(f32).astype(bf16)
     zero_tile = jnp.zeros((16, LOW), bf16)
@@ -314,14 +358,11 @@
     fold = group_rows // 16
 
     def build(it, carry):
-        keys = key_ref[pl.ds(pl.multiple_of(it * 8, 8), 8), :]
-        high = (keys >> 8).astype(f32)
-        low = (keys & 255).astype(f32)
         for k in range(0, 8, fold):
             made = []
             for kk in range(k, k + fold):
-                high_row = jnp.broadcast_to(high[kk : kk + 1, :], (16, LOW)).astype(bf16)
-                low_row = jnp.broadcast_to(low[kk : kk + 1, :], (16, LOW)).astype(bf16)
+                high_row = jnp.broadcast_to(key_high[kk, pl.ds(it, 1), :], (16, LOW)).astype(bf16)
+                low_row = jnp.broadcast_to(key_low[kk, pl.ds(it, 1), :], (16, LOW)).astype(bf16)
                 left = jnp.concatenate(
                     [
                         jnp.where(high_row == jnp.asarray(h, bf16), same_node, zero_tile)
@@ -343,15 +384,16 @@
                 )
         return carry
 
+    unscale_own = split_in_two(table1[...], first_own)
     lax.fori_loop(0, nodes // 128, build, 0)
 
     wait_weights(0)
     weight_lanes = (
         slice(0, 2 * LANE),
         weight_parts[1],
-        weight_parts[2],
+        slice(3 * LANE + 2 * hid, 3 * LANE + 4 * hid),
     )
-    small_full = wfull[:, 3 * LANE : 4 * LANE].astype(f32)
+    small_full = wfull[:, 2 * LANE : 3 * LANE].astype(f32)
     for v in range(6):
         vectors[v] = jnp.broadcast_to(small_full[:, v : v + 1], (hid, LANE))
 
@@ -407,6 +449,7 @@
         before[...] = dot(matrix(level), joined, NN)
         return joined, activate(level, keep_slope, kept_or_none(kept), off)
 
+    send_weights(1)
     def layer_one(i, carry):
         off = pl.multiple_of(i * block, block)
         own = dot(first_own[...], counts[pl.ds(off, block), 0:nodes], NT)
@@ -432,6 +475,8 @@
     def exchange_forward(table, x):
         pick_rows(table, outs)
         start_rows(outs, ins.at[x % 2], row_ssem.at[x + 1], row_rsem.at[x + 1])
+        if x == 0:
+            send_weights(2)
         own_sums(table)
         wait_rows(outs, ins.at[x % 2], row_ssem.at[x + 1], row_rsem.at[x + 1])
         table[:, nodes:] = ins[x % 2].T
@@ -460,7 +505,7 @@
     gfull[...] = jnp.zeros(gfull.shape, f32)
     gacc[...] = jnp.zeros(gacc.shape, f32)
     bacc[...] = jnp.zeros(bacc.shape, f32)
-    head_low = wfull[:, 2 * LANE : 3 * LANE]
+    head_low = wfull[:, 3 * LANE + 4 * hid :]
     cls_pad = round_up(cls, 16)
     one_over_count = 1.0 / label_count[0:1, 0:1]
     class_iota = lax.broadcasted_iota(i32, (cls_pad, block), 0)
@@ -912,18 +957,11 @@
         block=block,
         fin_pad=fin_pad,
         hid=hid,
+        cap=cap,
+        slots=slots,
         units=units,
         unit_rows=unit_rows,
     )
-
-    away = neighbours - nodes
-    source = away // cap
-    moved = nodes + source * pad + (away - source * cap)
-    mapped = jnp.where(away < 0, neighbours, moved)
-    live = lax.broadcasted_iota(i32, mapped.shape, 1) < degrees[:, None]
-    keys = jnp.where(live, mapped, -1).reshape(nodes // 16, 16 * slots)
-    send_padded = jnp.pad(send_rows, ((0, 0), (0, pad - cap)), constant_values=-1)
-    send_wide = jnp.broadcast_to(send_padded.reshape(remote, 1), (remote, LANE))
 
     vmem = pl.BlockSpec(memory_space=pltpu.VMEM)
     smem = pl.BlockSpec(memory_space=pltpu.SMEM)
@@ -934,6 +972,10 @@
     scratch = [
         pltpu.VMEM((nodes, columns), narrow),
         pltpu.VMEM((stored, nodes), narrow),
+        pltpu.VMEM((remote, LANE), i32),
+        pltpu.VMEM((nodes // LANE * slots, LANE), i32),
+        pltpu.VMEM((8, nodes // LANE, LOW), f32),
+        pltpu.VMEM((8, nodes // LANE, LOW), f32),
         pltpu.VMEM((fin_pad, nodes), bf16),
         pltpu.VMEM((hid, columns), bf16),
         pltpu.VMEM((hid, columns), bf16),
@@ -945,8 +987,6 @@
         pltpu.VMEM((hid, kept_nodes), f32),
         pltpu.VMEM((hid, nodes), bf16),
         pltpu.VMEM((hid, nodes), f32),
-        pltpu.VMEM((remote, fin_pad), bf16),
-        pltpu.VMEM((remote, fin_pad), bf16),
         pltpu.VMEM((remote, hid), bf16),
         pltpu.VMEM((2, remote, hid), bf16),
         pltpu.VMEM((8, nodes), f32),
@@ -1008,12 +1048,12 @@
         ),
     )(
         features.T,
-        keys,
+        neighbours.T,
         degrees.reshape(nodes // LANE, LANE),
         labels.reshape(nodes // LANE, LANE),
         train_mask.reshape(nodes // LANE, LANE),
         node_counts,
-        send_wide,
+        send_rows.T,
         weight_first.T,
         weight_rest.transpose(0, 2, 1),
         weight_head,

time: 121 us -> 116 us (0.959)
  local copies, waits for them, and re-layouts: 3.15 us -> 0 us
    reshape x1 -> x0, local copies, waits for them, and re-layouts: 1.53 us -> none  [per_device(): keys = jnp.where(live, mapped, -1).reshape(nodes // 16, 16 * slots)]
where the time goes in v3:
time: 116 us
  Pallas kernels  114 us (98%)
  between operations  1.47 us (1%)
    pallas_call x1, Pallas kernels, per_device(): pl.pallas_call(functools.partial(step_kernel, cfg), out_shape=(jax.ShapeD...  112 us
    pallas_call x1, Pallas kernels, per_device(): pl.pallas_call(functools.partial(update_kernel, fin, cls), out_shape=tupl...  2.35 us

profile of v3, /device:TPU:0, one launch (start us, length us, event | category | flops | bytes accessed | tf_op | source)
XLA Modules:
  0.0 115.9 jit_solution(10305097966737295785)
XLA Ops:
  1.3 112.0 %shard_map.373 = (f32[2,4,32,128]{3,2,1,0:T(8,128)}, f32[32,128]{1,0:T(8,128)}, f32[2,32,128]{2,1,0:T(8,128)}, f32[8,128]{1,0:T(8,128)}) custom-call(bf16[100,4096]{1,0:T(8,128)(2,1)} %bitcast.23, s32[16,4096]{1,0:T(8,128)} %bitcast.26, s32[32,128]{1,0:T(8,128)} %bitcast.33, s32[32,128]{1,0:T(8,128)} %bitcast.34, s32[32,128]{1,0:T(8,128)} %bitcast.35, ...), custom_call_target="tpu_custom_call" | custom-call | tf_op jit(solution)/shard_map/pallas_call | solution.py:1035
  113.4 2.3 %shard_map.374 = (f32[32,200]{1,0:T(8,128)}, f32[32,200]{1,0:T(8,128)}, f32[32,200]{1,0:T(8,128)}, f32[2,32,512]{2,1,0:T(8,128)}, f32[2,32,512]{2,1,0:T(8,128)},...) custom-call(f32[2,4,32,128]{3,2,1,0:T(8,128)} %get-tuple-element.46., ...), custom_call_target="tpu_custom_call" | custom-call | tf_op jit(solution)/shard_map/pallas_call | solution.py:1078

commit v4 on v3

--- a/solution.py
+++ b/solution.py
@@ -84,9 +84,9 @@
     wfull,
     vectors,
     before,
-    active,
     slope,
     ghid,
+    losses,
     gacc,
     bacc,
     gfull,
@@ -130,6 +130,7 @@
     my_group, my_shard = lax.axis_index("group"), lax.axis_index("shard")
     me = my_group * n_shard + my_shard
     blocks = nodes // block
+    streams, large = cfg["streams"], cfg["large"]
 
     def target(group, shard):
         return {"group": group, "shard": shard}
@@ -138,32 +139,46 @@
 
     barrier = pltpu.get_barrier_semaphore()
 
-    def greet(i, carry):
-        peer = lax.rem(me + i, devices)
+    def greet(group, shard):
         pl.semaphore_signal(
-            barrier,
-            inc=1,
-            device_id=target(lax.div(peer, n_shard), lax.rem(peer, n_shard)),
-            device_id_type=MESH,
+            barrier, inc=1, device_id=target(group, shard), device_id_type=MESH
         )
-        return carry
-
-    lax.fori_loop(1, devices, greet, 0)
+
+    def each_shard(action, group, first):
+        if n_shard <= 8:
+            for i in range(first, n_shard):
+                action(group, lax.rem(my_shard + i, n_shard))
+        else:
+
+            def run(i, carry):
+                action(group, lax.rem(my_shard + i, n_shard))
+                return carry
+
+            lax.fori_loop(first, n_shard, run, 0)
+
+    def each_group(action):
+        for i in range(1, n_group):
+            action(lax.rem(my_group + i, n_group), my_shard)
+
+    def each_device(action):
+        for i in range(n_group):
+            each_shard(action, lax.rem(my_group + i, n_group), 1 if i == 0 else 0)
+
+    each_device(greet)
 
     def start_rows(source, landing, ssem, rsem):
-        def start(i, carry):
-            peer = lax.rem(me + i, devices)
+        def start(group, shard):
+            peer = group * n_shard + shard
             pltpu.make_async_remote_copy(
                 src_ref=source.at[pl.ds(pl.multiple_of(peer * pad, pad), pad), :],
                 dst_ref=landing.at[pl.ds(pl.multiple_of(me * pad, pad), pad), :],
                 send_sem=ssem,
                 recv_sem=rsem,
-                device_id=target(lax.div(peer, n_shard), lax.rem(peer, n_shard)),
+                device_id=target(group, shard),
                 device_id_type=MESH,
             ).start()
-            return carry
-
-        lax.fori_loop(1, devices, start, 0)
+
+        each_device(start)
         own = pl.ds(pl.multiple_of(me * pad, pad), pad)
         landing[own, :] = source[own, :]
 
@@ -295,19 +310,17 @@
     def send_weights(part):
         lanes = weight_parts[part]
 
-        def start(i, carry):
-            shard = lax.rem(my_shard + i, n_shard)
+        def start(group, shard):
             pltpu.make_async_remote_copy(
                 src_ref=wsend.at[:, lanes],
                 dst_ref=wwire.at[own_chunk, lanes],
                 send_sem=w_ssem.at[part],
                 recv_sem=w_rsem.at[part],
-                device_id=target(my_group, shard),
+                device_id=target(group, shard),
                 device_id_type=MESH,
             ).start()
-            return carry
-
-        lax.fori_loop(1, n_shard, start, 0)
+
+        each_shard(start, my_group, 1)
 
     def wait_weights(part):
         lanes = weight_parts[part]
@@ -385,7 +398,9 @@
         return carry
 
     unscale_own = split_in_two(table1[...], first_own)
-    lax.fori_loop(0, nodes // 128, build, 0)
+    lax.fori_loop(0, nodes // 256, build, 0)
+    send_weights(1)
+    lax.fori_loop(nodes // 256, nodes // 128, build, 0)
 
     wait_weights(0)
     weight_lanes = (
@@ -416,67 +431,83 @@
     def fold_rows(value):
         return jnp.sum(value.reshape(STRIP // 8, 8, value.shape[1]), axis=0)
 
-    def activate(level, keep_slope, kept, off):
+    def activate(level, keep_slope, kept, off, w):
         squares = jnp.zeros((8, block), f32)
         for st in strips:
             if kept is not None and keep_slope:
                 b = kept[st, pl.ds(off, block)]
             else:
-                b = before[st, :] + twice(vectors[level, st, :], block)
+                b = before[w, st, :] + twice(vectors[level, st, :], block)
             if kept is not None and not keep_slope:
                 kept[st, pl.ds(off, block)] = b
             s = 0.5 + 0.5 * jnp.tanh(0.5 * b)
             a = b * s
-            active[st, :] = a
+            before[w, st, :] = a
             if keep_slope:
-                slope[st, :] = s + a * (1.0 - s)
+                slope[w, st, :] = s + a * (1.0 - s)
             squares = squares + fold_rows(a * a)
         mean_square = jnp.sum(squares, axis=0, keepdims=True) * (1.0 / hid)
         return lax.rsqrt(mean_square + norm_epsilon)
 
-    def hidden_strip(level, st, inverse):
-        return (twice(vectors[3 + level, st, :], block) * (active[st, :] * inverse)).astype(bf16)
+    def hidden_strip(level, st, inverse, w):
+        scaled = before[w, st, :] * inverse
+        return (twice(vectors[3 + level, st, :], block) * scaled).astype(bf16)
 
     def kept_or_none(kept):
         return kept if kept is not None and kept.shape[1] == nodes else None
 
-    def forward_block(level, off, summed, table, mean, kept, keep_slope):
+    def forward_block(level, off, summed, table, mean, kept, keep_slope, w):
         lanes = pl.ds(off, block)
         mean_low = (summed * info[0:1, lanes]).astype(bf16)
         if mean is not None:
             mean[:, lanes] = mean_low
         joined = jnp.concatenate([table[:, lanes], mean_low], axis=0)
-        before[...] = dot(matrix(level), joined, NN)
-        return joined, activate(level, keep_slope, kept_or_none(kept), off)
-
-    send_weights(1)
-    def layer_one(i, carry):
-        off = pl.multiple_of(i * block, block)
-        own = dot(first_own[...], counts[pl.ds(off, block), 0:nodes], NT)
-        away = dot(first_remote[...], counts[pl.ds(off, block), nodes:], NT)
+        before[w] = dot(matrix(level), joined, NN)
+        yield
+        return joined, activate(level, keep_slope, kept_or_none(kept), off, w)
+
+    def run_blocks(make):
+        def body(k, carry):
+            live = [
+                make(pl.multiple_of((k * streams + w) * block, block), w)
+                for w in range(streams)
+            ]
+            ended, tick = set(), 0
+            while len(ended) < streams:
+                for w in range(streams):
+                    if tick >= w and w not in ended:
+                        if next(live[w], "end") == "end":
+                            ended.add(w)
+                tick += 1
+            return carry
+
+        lax.fori_loop(0, blocks // streams, body, 0)
+
+    send_weights(2)
+    def layer_one(off, w):
+        rows = pl.ds(off, block)
+        own = dot(first_own[...], counts[rows, 0:nodes], NT)
+        away = dot(first_remote[...], counts[rows, nodes:], NT)
+        yield
         summed = joined_parts(own, unscale_own) + joined_parts(away, unscale_remote)
-        _, inverse = forward_block(0, off, summed, table1, mean1, before1, False)
+        _, inverse = yield from forward_block(0, off, summed, table1, mean1, before1, False, w)
+        yield
         for st in strips:
-            table2[st, pl.ds(off, block)] = hidden_strip(0, st, inverse)
-        return carry
-
-    lax.fori_loop(0, blocks, layer_one, 0)
+            table2[st, rows] = hidden_strip(0, st, inverse, w)
+
+    run_blocks(layer_one)
 
     def own_sums(table):
         def add(i, carry):
-            off = pl.multiple_of(i * block, block)
-            wide[:, pl.ds(off, block)] = dot(
-                table[:, 0:nodes], c_block(off, slice(0, nodes)), NT
-            )
+            rows = pl.ds(pl.multiple_of(i * large, large), large)
+            wide[:, rows] = dot(table[:, 0:nodes], counts[rows, 0:nodes].astype(bf16), NT)
             return carry
 
-        lax.fori_loop(0, blocks, add, 0)
+        lax.fori_loop(0, nodes // large, add, 0)
 
     def exchange_forward(table, x):
         pick_rows(table, outs)
         start_rows(outs, ins.at[x % 2], row_ssem.at[x + 1], row_rsem.at[x + 1])
-        if x == 0:
-            send_weights(2)
         own_sums(table)
         wait_rows(outs, ins.at[x % 2], row_ssem.at[x + 1], row_rsem.at[x + 1])
         table[:, nodes:] = ins[x % 2].T
@@ -489,14 +520,15 @@
     exchange_forward(table2, 0)
     wait_weights(1)
 
-    def layer_two(i, carry):
-        off = pl.multiple_of(i * block, block)
-        _, inverse = forward_block(1, off, all_sums(table2, off), table2, mean2, before2, False)
+    def layer_two(off, w):
+        summed = all_sums(table2, off)
+        yield
+        _, inverse = yield from forward_block(1, off, summed, table2, mean2, before2, False, w)
+        yield
         for st in strips:
-            table3[st, pl.ds(off, block)] = hidden_strip(1, st, inverse)
-        return carry
-
-    lax.fori_loop(0, blocks, layer_two, 0)
+            table3[st, pl.ds(off, block)] = hidden_strip(1, st, inverse, w)
+
+    run_blocks(layer_two)
 
     exchange_forward(table3, 1)
     wait_weights(2)
@@ -510,20 +542,20 @@
     one_over_count = 1.0 / label_count[0:1, 0:1]
     class_iota = lax.broadcasted_iota(i32, (cls_pad, block), 0)
 
-    def backward_block(level, off, joined, inverse, need_input):
+    def backward_block(level, off, joined, inverse, need_input, w):
         lanes = pl.ds(off, block)
         crossed = jnp.zeros((8, block), f32)
         for st in strips:
-            u = ghid[st, :] * twice(vectors[3 + level, st, :], block)
-            crossed = crossed + fold_rows(u * active[st, :])
+            u = ghid[w, st, :] * twice(vectors[3 + level, st, :], block)
+            crossed = crossed + fold_rows(u * before[w, st, :])
         factor = jnp.sum(crossed, axis=0, keepdims=True) * (1.0 / hid) * inverse
         factor = factor * inverse * inverse
         low_parts = []
         for st in strips:
-            g = ghid[st, :]
-            a = active[st, :]
+            g = ghid[w, st, :]
+            a = before[w, st, :]
             u = g * twice(vectors[3 + level, st, :], block)
-            low = ((inverse * u - a * factor) * slope[st, :]).astype(bf16)
+            low = ((inverse * u - a * factor) * slope[w, st, :]).astype(bf16)
             low_parts.append(low)
             gain_term = g * (a * inverse)
             bias_term = low.astype(f32)
@@ -535,6 +567,7 @@
             gacc[level, st, :] += gain_sum
             bacc[level, st, :] += bias_sum
         low = jnp.concatenate(low_parts, axis=0)
+        yield
         into = gfirst if level == 0 else gfull.at[level - 1]
         added = dot(low, joined, NT)
         for j in range(joined.shape[0] // LANE):
@@ -544,12 +577,17 @@
             wide[:, lanes] = back[0:hid, :]
             gmean[:, lanes] = (back[hid:, :] * info[0:1, lanes]).astype(bf16)
 
-    def layer_three(i, loss):
-        off = pl.multiple_of(i * block, block)
+    def layer_three(off, w):
         lanes = pl.ds(off, block)
-        joined, inverse = forward_block(2, off, all_sums(table3, off), table3, None, None, True)
-        last = jnp.concatenate([hidden_strip(2, st, inverse) for st in strips], axis=0)
+        summed = all_sums(table3, off)
+        yield
+        joined, inverse = yield from forward_block(
+            2, off, summed, table3, None, None, True, w
+        )
+        last = jnp.concatenate([hidden_strip(2, st, inverse, w) for st in strips], axis=0)
+        yield
         logits = dot(head_low, last, TN)[0:cls_pad, :]
+        yield
         logits = jnp.where(class_iota < cls, logits, -jnp.inf)
         highest = jnp.max(logits, axis=0, keepdims=True)
         shifted = logits - highest
@@ -558,35 +596,35 @@
         hot = class_iota == info[1:2, lanes].astype(i32)
         counted = info[2:3, lanes]
         chosen = jnp.sum(jnp.where(hot, shifted, 0.0), axis=0, keepdims=True)
-        loss = loss + (jnp.log(total) - chosen) * counted
-        g_logits = (grown / total - jnp.where(hot, 1.0, 0.0)) * (counted * one_over_count)
+        losses[w : w + 1, :] += (jnp.log(total) - chosen) * counted
+        g_logits = (grown * (1.0 / total) - jnp.where(hot, 1.0, 0.0)) * (counted * one_over_count)
         g_low = jnp.concatenate(
             [g_logits, jnp.zeros((LANE - cls_pad, block), f32)], axis=0
         ).astype(bf16)
+        yield
         ghead[...] += dot(last, g_low, NT)
-        ghid[...] = dot(head_low, g_low, NN)
-        backward_block(2, off, joined, inverse, True)
-        return loss
-
-    loss = lax.fori_loop(0, blocks, layer_three, jnp.zeros((1, block), f32))
+        ghid[w] = dot(head_low, g_low, NN)
+        yield
+        yield from backward_block(2, off, joined, inverse, True, w)
+
+    losses[...] = jnp.zeros(losses.shape, f32)
+    run_blocks(layer_three)
 
     def start_first(seg):
         for piece in range(n_group):
             gwire[seg, piece] = gfull[seg, piece].astype(wire)
 
-        def start(i, carry):
-            group = lax.rem(my_group + i, n_group)
+        def start(group, shard):
             pltpu.make_async_remote_copy(
                 src_ref=gwire.at[seg, group],
                 dst_ref=recv1.at[seg, my_group],
                 send_sem=g_ssem.at[0, seg],
                 recv_sem=g_rsem.at[0, seg],
-                device_id=target(group, my_shard),
+                device_id=target(group, shard),
                 device_id_type=MESH,
             ).start()
-            return carry
-
-        lax.fori_loop(1, n_group, start, 0)
+
+        each_group(start)
         recv1[seg, my_group] = jnp.zeros(recv1.shape[2:], wire)
 
     def start_second(seg):
@@ -598,19 +636,17 @@
         gfull[seg, my_group] = total
         send2[seg] = total.astype(wire).reshape(n_shard, chunk, LANE)
 
-        def start(i, carry):
-            shard = lax.rem(my_shard + i, n_shard)
+        def start(group, shard):
             pltpu.make_async_remote_copy(
                 src_ref=send2.at[seg, shard],
                 dst_ref=recv2.at[seg, my_shard],
                 send_sem=g_ssem.at[1, seg],
                 recv_sem=g_rsem.at[1, seg],
-                device_id=target(my_group, shard),
+                device_id=target(group, shard),
                 device_id_type=MESH,
             ).start()
-            return carry
-
-        lax.fori_loop(1, n_shard, start, 0)
+
+        each_shard(start, my_group, 1)
         recv2[seg, my_shard] = jnp.zeros(recv2.shape[2:], wire)
 
     def start_third(seg):
@@ -621,19 +657,17 @@
             total = total + recv2[seg, shard].astype(f32)
         part3[seg] = total
 
-        def start(i, carry):
-            group = lax.rem(my_group + i, n_group)
+        def start(group, shard):
             pltpu.make_async_remote_copy(
                 src_ref=part3.at[seg],
                 dst_ref=recv3.at[seg, my_group],
                 send_sem=g_ssem.at[2, seg],
                 recv_sem=g_rsem.at[2, seg],
-                device_id=target(group, my_shard),
+                device_id=target(group, shard),
                 device_id_type=MESH,
             ).start()
-            return carry
-
-        lax.fori_loop(1, n_group, start, 0)
+
+        each_group(start)
         recv3[seg, my_group] = total
         return jnp.sum(total * total)
 
@@ -659,19 +693,17 @@
         ghead[...] = total
         hwire[...] = total.astype(wire).reshape(n_shard, chunk, LANE)
 
-        def start(i, carry):
-            shard = lax.rem(my_shard + i, n_shard)
+        def start(group, shard):
             pltpu.make_async_remote_copy(
                 src_ref=hwire.at[shard],
                 dst_ref=hrecv.at[my_shard],
                 send_sem=h_ssem.at[0],
                 recv_sem=h_rsem.at[0],
-                device_id=target(my_group, shard),
+                device_id=target(group, shard),
                 device_id_type=MESH,
             ).start()
-            return carry
-
-        lax.fori_loop(1, n_shard, start, 0)
+
+        each_shard(start, my_group, 1)
         hrecv[my_shard] = jnp.zeros(hrecv.shape[1:], wire)
 
     def share_head():
@@ -682,19 +714,17 @@
             total = total + hrecv[shard].astype(f32)
         hpart[...] = total
 
-        def start(i, carry):
-            group = lax.rem(my_group + i, n_group)
+        def start(group, shard):
             pltpu.make_async_remote_copy(
                 src_ref=hpart,
                 dst_ref=hfinal.at[my_group],
                 send_sem=h_ssem.at[1],
                 recv_sem=h_rsem.at[1],
-                device_id=target(group, my_shard),
+                device_id=target(group, shard),
                 device_id_type=MESH,
             ).start()
-            return carry
-
-        lax.fori_loop(1, n_group, start, 0)
+
+        each_group(start)
         hfinal[my_group] = total
 
     def wait_head():
@@ -715,9 +745,7 @@
             whole = gfirst[tile].reshape(n_shard, chunk, LANE)
             fwire[unit] = whole[:, part * unit_rows : (part + 1) * unit_rows, :].astype(wire)
 
-        def start(i, carry):
-            peer = lax.rem(me + i, devices)
-            group, shard = lax.div(peer, n_shard), lax.rem(peer, n_shard)
+        def start(group, shard):
             pltpu.make_async_remote_copy(
                 src_ref=fwire.at[lax.rem(group, units), shard],
                 dst_ref=frecv.at[me],
@@ -726,9 +754,8 @@
                 device_id=target(group, shard),
                 device_id_type=MESH,
             ).start()
-            return carry
-
-        lax.fori_loop(1, devices, start, 0)
+
+        each_device(start)
         frecv[me] = fwire[lax.rem(my_group, units), my_shard]
 
     def share_first_layer():
@@ -737,19 +764,17 @@
         total = jnp.sum(frecv[...].astype(f32), axis=0)
         fpart[...] = total
 
-        def start(i, carry):
-            group = lax.rem(my_group + i, n_group)
+        def start(group, shard):
             pltpu.make_async_remote_copy(
                 src_ref=fpart,
                 dst_ref=ffinal.at[my_group],
                 send_sem=f_ssem.at[1],
                 recv_sem=f_rsem.at[1],
-                device_id=target(group, my_shard),
+                device_id=target(group, shard),
                 device_id_type=MESH,
             ).start()
-            return carry
-
-        lax.fori_loop(1, n_group, start, 0)
+
+        each_group(start)
         ffinal[my_group] = total
         return jnp.sum(total * total) * (units / n_group)
 
@@ -769,12 +794,11 @@
         meanwhile()
 
         def add(i, carry):
-            off = pl.multiple_of(i * block, block)
-            lanes = pl.ds(off, block)
+            lanes = pl.ds(pl.multiple_of(i * large, large), large)
             wide[:, lanes] += dot(gmean[...], counts[:, lanes].astype(bf16), NN)
             return carry
 
-        lax.fori_loop(0, blocks, add, 0)
+        lax.fori_loop(0, nodes // large, add, 0)
         wait_rows(outs, ins.at[x % 2], row_ssem.at[x + 1], row_rsem.at[x + 1])
 
     def returned(x, off):
@@ -786,18 +810,17 @@
     exchange_backward(2, lambda: start_first(1))
     start_second(1)
 
-    def backward_two(i, carry):
-        off = pl.multiple_of(i * block, block)
+    def backward_two(off, w):
         lanes = pl.ds(off, block)
-        ghid[...] = returned(2, off)
+        ghid[w] = returned(2, off)
         joined = jnp.concatenate([table2[:, lanes], mean2[:, lanes]], axis=0)
         if before2.shape[1] < nodes:
-            before[...] = dot(matrix(1), joined, NN)
-        inverse = activate(1, True, kept_or_none(before2), off)
-        backward_block(1, off, joined, inverse, True)
-        return carry
-
-    lax.fori_loop(0, blocks, backward_two, 0)
+            before[w] = dot(matrix(1), joined, NN)
+        yield
+        inverse = activate(1, True, kept_or_none(before2), off, w)
+        yield from backward_block(1, off, joined, inverse, True, w)
+
+    run_blocks(backward_two)
 
     def meanwhile():
         start_first(0)
@@ -808,39 +831,36 @@
     start_second(0)
     share_head()
 
-    def backward_one(i, carry):
-        off = pl.multiple_of(i * block, block)
+    def backward_one(off, w):
         lanes = pl.ds(off, block)
-        ghid[...] = returned(3, off)
+        ghid[w] = returned(3, off)
         joined = jnp.concatenate([table1[:, lanes], mean1[:, lanes]], axis=0)
         if before1.shape[1] < nodes:
-            before[...] = dot(matrix(0), joined, NN)
-        inverse = activate(0, True, kept_or_none(before1), off)
-        backward_block(0, off, joined, inverse, False)
-        return carry
-
-    lax.fori_loop(0, blocks, backward_one, 0)
+            before[w] = dot(matrix(0), joined, NN)
+        yield
+        inverse = activate(0, True, kept_or_none(before1), off, w)
+        yield from backward_block(0, off, joined, inverse, False, w)
+
+    run_blocks(backward_one)
     start_first_layer()
     square = square + start_third(0) + wait_head()
     square = square + share_first_layer()
 
     lane_of = lax.broadcasted_iota(i32, (8, LANE), 1)
-    mine = jnp.where(lane_of == 0, square, jnp.where(lane_of == 1, jnp.sum(loss), 0.0))
+    mine = jnp.where(lane_of == 0, square, jnp.where(lane_of == 1, jnp.sum(losses[...]), 0.0))
     scal_send[...] = mine
 
-    def send_scalars(i, carry):
-        peer = lax.rem(me + i, devices)
+    def send_scalars(group, shard):
         pltpu.make_async_remote_copy(
             src_ref=scal_send.at[pl.ds(0, 1), :],
             dst_ref=scal_recv.at[pl.ds(me, 1), :],
             send_sem=s_ssem,
             recv_sem=s_rsem,
-            device_id=target(lax.div(peer, n_shard), lax.rem(peer, n_shard)),
+            device_id=target(group, shard),
             device_id_type=MESH,
         ).start()
-        return carry
-
-    lax.fori_loop(1, devices, send_scalars, 0)
+
+    each_device(send_scalars)
     scal_recv[pl.ds(me, 1), :] = mine[0:1, :]
     for seg in range(2):
         wait_third(seg)
@@ -938,7 +958,8 @@
     pad = round_up(cap + 2, 16)
     remote = devices * pad
     columns = nodes + remote
-    block = 1024 if remote <= 512 else 512
+    roomy = remote <= 512
+    block, streams, large = (1024, 2, 2048) if roomy else (512, 1, 512)
     wire = bf16 if chunk % 16 == 0 else f32
     least = 16 if wire == bf16 else 8
     units = n_group if chunk * 2 // n_group >= least else 2
@@ -955,6 +976,8 @@
         chunk=chunk,
         wire=wire,
         block=block,
+        streams=streams,
+        large=large,
         fin_pad=fin_pad,
         hid=hid,
         cap=cap,
@@ -983,7 +1006,7 @@
         pltpu.VMEM((2 * fin_pad, remote), narrow),
         pltpu.VMEM((fin_pad, nodes), bf16),
         pltpu.VMEM((hid, nodes), bf16),
-        pltpu.VMEM((hid, kept_nodes), f32),
+        pltpu.VMEM((hid, LANE), f32),
         pltpu.VMEM((hid, kept_nodes), f32),
         pltpu.VMEM((hid, nodes), bf16),
         pltpu.VMEM((hid, nodes), f32),
@@ -994,10 +1017,10 @@
         pltpu.VMEM((hid, width), wire),
         pltpu.VMEM((hid, width), bf16),
         pltpu.VMEM((6, hid, LANE), f32),
-        pltpu.VMEM((hid, block), f32),
-        pltpu.VMEM((hid, block), f32),
-        pltpu.VMEM((hid, block), f32),
-        pltpu.VMEM((hid, block), f32),
+        pltpu.VMEM((streams, hid, block), f32),
+        pltpu.VMEM((streams, hid, block), f32),
+        pltpu.VMEM((streams, hid, block), f32),
+        pltpu.VMEM((8, block), f32),
         pltpu.VMEM((3, hid, LANE), f32),
         pltpu.VMEM((3, hid, LANE), f32),
         pltpu.VMEM((2, n_group, hid, LANE), f32),

time: 116 us -> 110 us (0.948)
  Pallas kernels: 114 us -> 109 us
    pallas_call x1, Pallas kernels: 112 us -> 106 us  [per_device(): pl.pallas_call(functools.partial(step_kernel, cfg), out_shape=(jax.ShapeD...]
where the time goes in v4:
time: 110 us
  Pallas kernels  109 us (99%)
  between operations  1.49 us (1%)
    pallas_call x1, Pallas kernels, per_device(): pl.pallas_call(functools.partial(step_kernel, cfg), out_shape=(jax.ShapeD...  106 us
    pallas_call x1, Pallas kernels, per_device(): pl.pallas_call(functools.partial(update_kernel, fin, cls), out_shape=tupl...  2.35 us

profile of v4, /device:TPU:0, one launch (start us, length us, event | category | flops | bytes accessed | tf_op | source)
XLA Modules:
  0.0 110.2 jit_solution(4378087169966762267)
XLA Ops:
  1.3 106.3 %shard_map.373 = (f32[2,4,32,128]{3,2,1,0:T(8,128)}, f32[32,128]{1,0:T(8,128)}, f32[2,32,128]{2,1,0:T(8,128)}, f32[8,128]{1,0:T(8,128)}) custom-call(bf16[100,4096]{1,0:T(8,128)(2,1)} %bitcast.23, s32[16,4096]{1,0:T(8,128)} %bitcast.26, s32[32,128]{1,0:T(8,128)} %bitcast.33, s32[32,128]{1,0:T(8,128)} %bitcast.34, s32[32,128]{1,0:T(8,128)} %bitcast.35, ...), custom_call_target="tpu_custom_call" | custom-call | tf_op jit(solution)/shard_map/pallas_call | solution.py:1058
  107.6 2.3 %shard_map.374 = (f32[32,200]{1,0:T(8,128)}, f32[32,200]{1,0:T(8,128)}, f32[32,200]{1,0:T(8,128)}, f32[2,32,512]{2,1,0:T(8,128)}, f32[2,32,512]{2,1,0:T(8,128)},...) custom-call(f32[2,4,32,128]{3,2,1,0:T(8,128)} %get-tuple-element.46., ...), custom_call_target="tpu_custom_call" | custom-call | tf_op jit(solution)/shard_map/pallas_call | solution.py:1101

commit v5 on v4

--- a/solution.py
+++ b/solution.py
@@ -269,8 +269,14 @@
         place = lax.rem(lax.broadcasted_iota(i32, (some, 2 * pad), 0), pad)
         found = jnp.where(lanes < pad, 256.0 * found, found)
         found = jnp.where(lax.rem(lanes, pad) == place, found, 0.0)
-        column = jnp.sum(found, axis=1, keepdims=True).astype(i32)
-        send_columns[rows, :] = jnp.broadcast_to(column, (some, LANE))
+        column = jnp.sum(found, axis=1, keepdims=True)
+        if picked.shape[0] == remote:
+            high = jnp.floor(column * (1.0 / LOW))
+            low = column - LOW * high
+            send_columns[0] = jnp.broadcast_to(high, (remote, LANE)).astype(bf16)
+            send_columns[1] = jnp.broadcast_to(low, (remote, LANE)).astype(bf16)
+        else:
+            send_columns[rows, :] = jnp.broadcast_to(column.astype(i32), (some, LANE))
 
     wsend[...] = jnp.zeros(wsend.shape, wire)
     wsend[:, 0:fin] = first_ref[:, 0:fin].astype(bf16).astype(wire)
@@ -286,12 +292,20 @@
 
     if picked.shape[0] == remote:
 
+        low_lane = lax.broadcasted_iota(i32, (remote, LANE), 1).astype(f32)
+        low_lanes = [(low_lane + LANE * half).astype(bf16) for half in range(LOW // LANE)]
+        none, one_pick = jnp.zeros((remote, LANE), bf16), jnp.ones((remote, LANE), bf16)
+
         def store_picks(i, carry):
-            off = pl.multiple_of(i * 512, 512)
-            picked[:, pl.ds(off, 512)] = make_picks(row_parts[0], off, 512).astype(narrow)
+            here = jnp.full((remote, LANE), i.astype(f32)).astype(bf16)
+            low = jnp.where(send_columns[0] == here, send_columns[1], none - 1)
+            for half in range(LOW // LANE):
+                lanes = pl.ds(pl.multiple_of(i * LOW + half * LANE, LANE), LANE)
+                found = jnp.where(low == low_lanes[half], one_pick, none)
+                picked[:, lanes] = found.astype(narrow)
             return carry
 
-        lax.fori_loop(0, nodes // 512, store_picks, 0)
+        lax.fori_loop(0, nodes // LOW, store_picks, 0)
 
     pick_rows(table1, out1)
     spare = lax.rem(lax.broadcasted_iota(i32, (remote, fin_pad), 0), pad)
@@ -398,6 +412,11 @@
         return carry
 
     unscale_own = split_in_two(table1[...], first_own)
+    spare_rows = slice(fin // 16 * 16, fin // 16 * 16 + 16)
+    ones_row = lax.broadcasted_iota(i32, (16, nodes), 0) == fin % 16
+    table1[spare_rows, :] = jnp.where(ones_row, 1.0, table1[spare_rows, :].astype(f32)).astype(
+        bf16
+    )
     lax.fori_loop(0, nodes // 256, build, 0)
     send_weights(1)
     lax.fori_loop(nodes // 256, nodes // 128, build, 0)
@@ -435,11 +454,11 @@
         squares = jnp.zeros((8, block), f32)
         for st in strips:
             if kept is not None and keep_slope:
-                b = kept[st, pl.ds(off, block)]
+                b = kept[st, pl.ds(off, block)].astype(f32)
             else:
                 b = before[w, st, :] + twice(vectors[level, st, :], block)
             if kept is not None and not keep_slope:
-                kept[st, pl.ds(off, block)] = b
+                kept[st, pl.ds(off, block)] = b.astype(kept.dtype)
             s = 0.5 + 0.5 * jnp.tanh(0.5 * b)
             a = b * s
             before[w, st, :] = a
@@ -546,26 +565,18 @@
         lanes = pl.ds(off, block)
         crossed = jnp.zeros((8, block), f32)
         for st in strips:
-            u = ghid[w, st, :] * twice(vectors[3 + level, st, :], block)
-            crossed = crossed + fold_rows(u * before[w, st, :])
-        factor = jnp.sum(crossed, axis=0, keepdims=True) * (1.0 / hid) * inverse
-        factor = factor * inverse * inverse
+            gain_term = ghid[w, st, :] * (before[w, st, :] * inverse)
+            crossed = crossed + fold_rows(gain_term * twice(vectors[3 + level, st, :], block))
+            gain_sum = gain_term[:, 0:LANE]
+            for j in range(1, block // LANE):
+                gain_sum = gain_sum + gain_term[:, j * LANE : (j + 1) * LANE]
+            gacc[level, st, :] += gain_sum
+        factor = jnp.sum(crossed, axis=0, keepdims=True) * (1.0 / hid) * inverse * inverse
         low_parts = []
         for st in strips:
-            g = ghid[w, st, :]
-            a = before[w, st, :]
-            u = g * twice(vectors[3 + level, st, :], block)
-            low = ((inverse * u - a * factor) * slope[w, st, :]).astype(bf16)
-            low_parts.append(low)
-            gain_term = g * (a * inverse)
-            bias_term = low.astype(f32)
-            gain_sum = gain_term[:, 0:LANE]
-            bias_sum = bias_term[:, 0:LANE]
-            for j in range(1, block // LANE):
-                gain_sum = gain_sum + gain_term[:, j * LANE : (j + 1) * LANE]
-                bias_sum = bias_sum + bias_term[:, j * LANE : (j + 1) * LANE]
-            gacc[level, st, :] += gain_sum
-            bacc[level, st, :] += bias_sum
+            u = ghid[w, st, :] * twice(vectors[3 + level, st, :], block)
+            low = (inverse * u - before[w, st, :] * factor) * slope[w, st, :]
+            low_parts.append(low.astype(bf16))
         low = jnp.concatenate(low_parts, axis=0)
         yield
         into = gfirst if level == 0 else gfull.at[level - 1]
@@ -573,6 +584,7 @@
         for j in range(joined.shape[0] // LANE):
             into[j] += added[:, j * LANE : (j + 1) * LANE]
         if need_input:
+            bacc[level - 1] += dot(low, jnp.ones((LANE, block), bf16), NT)
             back = dot(matrix(level), low, TN)
             wide[:, lanes] = back[0:hid, :]
             gmean[:, lanes] = (back[hid:, :] * info[0:1, lanes]).astype(bf16)
@@ -669,7 +681,7 @@
 
         each_group(start)
         recv3[seg, my_group] = total
-        return jnp.sum(total * total)
+        return jnp.sum(total * total, axis=0, keepdims=True)
 
     def wait_third(seg):
         for _ in range(n_group - 1):
@@ -680,12 +692,10 @@
         lane_wide = lax.broadcasted_iota(i32, (hid, LANE), 1)
         total = jnp.zeros((hid, LANE), f32)
         for n, level in enumerate(levels):
-            for acc, shift in ((bacc, 0), (gacc, len(levels))):
-                total = jnp.where(
-                    lane_wide == first_lane + shift + n,
-                    jnp.sum(acc[level], axis=1, keepdims=True),
-                    total,
-                )
+            found = jnp.sum(gacc[level], axis=1, keepdims=True)
+            total = jnp.where(lane_wide == first_lane + len(levels) + n, found, total)
+            if level > 0:
+                total = jnp.where(lane_wide == first_lane + n, bacc[level - 1], total)
         return total
 
     def start_head():
@@ -734,7 +744,7 @@
         for group in range(1, n_group):
             total = total + hfinal[group]
         head_out[...] = total
-        return jnp.sum(total * total) * (1.0 / n_group)
+        return jnp.sum(total * total, axis=0, keepdims=True) * (1.0 / n_group)
 
     units, unit_rows, row_parts_first = cfg["units"], cfg["unit_rows"], cfg["units"] // 2
 
@@ -776,7 +786,7 @@
 
         each_group(start)
         ffinal[my_group] = total
-        return jnp.sum(total * total) * (units / n_group)
+        return jnp.sum(total * total, axis=0, keepdims=True) * (units / n_group)
 
     def wait_first_layer():
         wait_bytes(ffinal.at[pl.ds(0, n_group - 1)], f_ssem.at[1])
@@ -846,14 +856,16 @@
     square = square + start_third(0) + wait_head()
     square = square + share_first_layer()
 
-    lane_of = lax.broadcasted_iota(i32, (8, LANE), 1)
-    mine = jnp.where(lane_of == 0, square, jnp.where(lane_of == 1, jnp.sum(losses[...]), 0.0))
+    row_of = lax.broadcasted_iota(i32, (8, LANE), 0)
+    loss_row = jnp.sum(losses[...], axis=0, keepdims=True)
+    loss_row = sum(loss_row[:, j * LANE : (j + 1) * LANE] for j in range(block // LANE))
+    mine = jnp.where(row_of == 0, square, jnp.where(row_of == 1, loss_row, 0.0))
     scal_send[...] = mine
 
     def send_scalars(group, shard):
         pltpu.make_async_remote_copy(
-            src_ref=scal_send.at[pl.ds(0, 1), :],
-            dst_ref=scal_recv.at[pl.ds(me, 1), :],
+            src_ref=scal_send.at[pl.ds(0, 2), :],
+            dst_ref=scal_recv.at[me, pl.ds(0, 2), :],
             send_sem=s_ssem,
             recv_sem=s_rsem,
             device_id=target(group, shard),
@@ -861,15 +873,17 @@
         ).start()
 
     each_device(send_scalars)
-    scal_recv[pl.ds(me, 1), :] = mine[0:1, :]
+    scal_recv[me] = mine
     for seg in range(2):
         wait_third(seg)
     part_out[...] = recv3[...]
     wait_first_layer()
-    wait_bytes(scal_recv.at[pl.ds(0, devices - 1), :], s_rsem)
-    wait_bytes(scal_recv.at[pl.ds(0, devices - 1), :], s_ssem)
-    totals = jnp.sum(scal_recv[...], axis=0, keepdims=True)
-    scalar_out[...] = jnp.where(lane_of == 2, label_count[0:1, 0:1], totals)
+    others = scal_recv.at[pl.ds(0, devices - 1), pl.ds(0, 2), :]
+    wait_bytes(others, s_rsem)
+    wait_bytes(others, s_ssem)
+    totals = jnp.sum(scal_recv[:, 0:2, :], axis=0)
+    scalar_out[0:2, :] = totals
+    scalar_out[2:3, :] = label_count
 
 
 def adamw(weight, grad, moment, square, rate, decay):
@@ -888,9 +902,9 @@
     outs = [refs[15 + 3 * k : 18 + 3 * k] for k in range(5)]
     copies = refs[30:33]
     loss_out, count_out, norm_out = refs[33:36]
-    norm = jnp.sqrt(scalar_ref[0:1, 0:1])
-    loss_out[...] = scalar_ref[0:1, 1:2]
-    count_out[...] = scalar_ref[0:1, 2:3]
+    norm = jnp.sqrt(jnp.sum(scalar_ref[0:1, :], axis=1, keepdims=True))
+    loss_out[...] = jnp.sum(scalar_ref[1:2, :], axis=1, keepdims=True)
+    count_out[...] = scalar_ref[2:3, 0:1]
     norm_out[...] = norm
     factor = jnp.minimum(1.0, threshold / norm)
     small_last = head_ref[...].T
@@ -995,7 +1009,7 @@
     scratch = [
         pltpu.VMEM((nodes, columns), narrow),
         pltpu.VMEM((stored, nodes), narrow),
-        pltpu.VMEM((remote, LANE), i32),
+        pltpu.VMEM((2, remote, LANE), bf16) if roomy else pltpu.VMEM((remote, LANE), i32),
         pltpu.VMEM((nodes // LANE * slots, LANE), i32),
         pltpu.VMEM((8, nodes // LANE, LOW), f32),
         pltpu.VMEM((8, nodes // LANE, LOW), f32),
@@ -1006,7 +1020,7 @@
         pltpu.VMEM((2 * fin_pad, remote), narrow),
         pltpu.VMEM((fin_pad, nodes), bf16),
         pltpu.VMEM((hid, nodes), bf16),
-        pltpu.VMEM((hid, LANE), f32),
+        pltpu.VMEM((hid, kept_nodes), bf16),
         pltpu.VMEM((hid, kept_nodes), f32),
         pltpu.VMEM((hid, nodes), bf16),
         pltpu.VMEM((hid, nodes), f32),
@@ -1022,7 +1036,7 @@
         pltpu.VMEM((streams, hid, block), f32),
         pltpu.VMEM((8, block), f32),
         pltpu.VMEM((3, hid, LANE), f32),
-        pltpu.VMEM((3, hid, LANE), f32),
+        pltpu.VMEM((2, hid, LANE), f32),
         pltpu.VMEM((2, n_group, hid, LANE), f32),
         pltpu.VMEM((2, n_group, hid, LANE), wire),
         pltpu.VMEM((2, n_group, hid, LANE), wire),
@@ -1041,7 +1055,7 @@
         pltpu.VMEM((chunk, LANE), f32),
         pltpu.VMEM((n_group, chunk, LANE), f32),
         pltpu.VMEM((8, LANE), f32),
-        pltpu.VMEM((devices, LANE), f32),
+        pltpu.VMEM((devices, 8, LANE), f32),
         dma((5,)),
         dma((5,)),
         dma((3,)),

time: 110 us -> 109 us (level)
    pallas_call x1, Pallas kernels: 106 us -> 105 us  [per_device(): pl.pallas_call(functools.partial(step_kernel, cfg), out_shape=(jax.ShapeD...]
where the time goes in v5:
time: 109 us
  Pallas kernels  108 us (99%)
  between operations  1.49 us (1%)
    pallas_call x1, Pallas kernels, per_device(): pl.pallas_call(functools.partial(step_kernel, cfg), out_shape=(jax.ShapeD...  105 us
    pallas_call x1, Pallas kernels, per_device(): pl.pallas_call(functools.partial(update_kernel, fin, cls), out_shape=tupl...  2.4 us

profile of v5, /device:TPU:0, one launch (start us, length us, event | category | flops | bytes accessed | tf_op | source)
XLA Modules:
  0.0 109.1 jit_solution(1690691401939613435)
XLA Ops:
  1.3 105.2 %shard_map.373 = (f32[2,4,32,128]{3,2,1,0:T(8,128)}, f32[32,128]{1,0:T(8,128)}, f32[2,32,128]{2,1,0:T(8,128)}, f32[8,128]{1,0:T(8,128)}) custom-call(bf16[100,4096]{1,0:T(8,128)(2,1)} %bitcast.23, s32[16,4096]{1,0:T(8,128)} %bitcast.26, s32[32,128]{1,0:T(8,128)} %bitcast.33, s32[32,128]{1,0:T(8,128)} %bitcast.34, s32[32,128]{1,0:T(8,128)} %bitcast.35, ...), custom_call_target="tpu_custom_call" | custom-call | tf_op jit(solution)/shard_map/pallas_call | solution.py:1072
  106.5 2.4 %shard_map.374 = (f32[32,200]{1,0:T(8,128)}, f32[32,200]{1,0:T(8,128)}, f32[32,200]{1,0:T(8,128)}, f32[2,32,512]{2,1,0:T(8,128)}, f32[2,32,512]{2,1,0:T(8,128)},...) custom-call(f32[2,4,32,128]{3,2,1,0:T(8,128)} %get-tuple-element.46., ...), custom_call_target="tpu_custom_call" | custom-call | tf_op jit(solution)/shard_map/pallas_call | solution.py:1115

commit v6 on v5

--- a/solution.py
+++ b/solution.py
@@ -343,6 +343,13 @@
         wait_bytes(wwire.at[rows, lanes], w_ssem.at[part])
         wfull[:, lanes] = wwire[:, lanes].astype(bf16)
 
+    gfirst[...] = jnp.zeros(gfirst.shape, f32)
+    ghead[...] = jnp.zeros(ghead.shape, f32)
+    gfull[...] = jnp.zeros(gfull.shape, f32)
+    gacc[...] = jnp.zeros(gacc.shape, f32)
+    bacc[...] = jnp.zeros(bacc.shape, f32)
+    losses[...] = jnp.zeros(losses.shape, f32)
+
     pl.semaphore_wait(barrier, devices - 1)
     start_rows(out1, in1, row_ssem.at[0], row_rsem.at[0])
     wwire[own_chunk, :] = wsend[...]
@@ -551,11 +558,6 @@
 
     exchange_forward(table3, 1)
     wait_weights(2)
-    gfirst[...] = jnp.zeros(gfirst.shape, f32)
-    ghead[...] = jnp.zeros(ghead.shape, f32)
-    gfull[...] = jnp.zeros(gfull.shape, f32)
-    gacc[...] = jnp.zeros(gacc.shape, f32)
-    bacc[...] = jnp.zeros(bacc.shape, f32)
     head_low = wfull[:, 3 * LANE + 4 * hid :]
     cls_pad = round_up(cls, 16)
     one_over_count = 1.0 / label_count[0:1, 0:1]
@@ -619,7 +621,6 @@
         yield
         yield from backward_block(2, off, joined, inverse, True, w)
 
-    losses[...] = jnp.zeros(losses.shape, f32)
     run_blocks(layer_three)
 
     def start_first(seg):

time: 109 us -> 109 us (level)
  no operation moved by 1% of the time
where the time goes in v6:
time: 109 us
  Pallas kernels  107 us (98%)
  between operations  1.49 us (1%)
    pallas_call x1, Pallas kernels, per_device(): pl.pallas_call(functools.partial(step_kernel, cfg), out_shape=(jax.ShapeD...  105 us
    pallas_call x1, Pallas kernels, per_device(): pl.pallas_call(functools.partial(update_kernel, fin, cls), out_shape=tupl...  2.4 us

profile of v6, /device:TPU:0, one launch (start us, length us, event | category | flops | bytes accessed | tf_op | source)
XLA Modules:
  0.0 109.0 jit_solution(6206275354355146762)
XLA Ops:
  1.3 105.1 %shard_map.373 = (f32[2,4,32,128]{3,2,1,0:T(8,128)}, f32[32,128]{1,0:T(8,128)}, f32[2,32,128]{2,1,0:T(8,128)}, f32[8,128]{1,0:T(8,128)}) custom-call(bf16[100,4096]{1,0:T(8,128)(2,1)} %bitcast.23, s32[16,4096]{1,0:T(8,128)} %bitcast.26, s32[32,128]{1,0:T(8,128)} %bitcast.33, s32[32,128]{1,0:T(8,128)} %bitcast.34, s32[32,128]{1,0:T(8,128)} %bitcast.35, ...), custom_call_target="tpu_custom_call" | custom-call | tf_op jit(solution)/shard_map/pallas_call | solution.py:1073
  106.4 2.4 %shard_map.374 = (f32[32,200]{1,0:T(8,128)}, f32[32,200]{1,0:T(8,128)}, f32[32,200]{1,0:T(8,128)}, f32[2,32,512]{2,1,0:T(8,128)}, f32[2,32,512]{2,1,0:T(8,128)},...) custom-call(f32[2,4,32,128]{3,2,1,0:T(8,128)} %get-tuple-element.46., ...), custom_call_target="tpu_custom_call" | custom-call | tf_op jit(solution)/shard_map/pallas_call | solution.py:1116
